TPU v7x, 128 devices: a whole 4x4x4 slice. The times are simulated.
128 devices in a mesh: gx: 16 (over y, x_hi, core), gy: 8 (over z, x_lo).
Axes of the slice: x: 4 (x_hi: 2, x_lo: 2; x = x_hi * 2 + x_lo), y: 4, z: 4, core: 2. Of those that a mesh axis runs over, the one named last changes fastest.
Arguments:
- obj: float32 [2, 4096, 8192], P(None, 'gy', 'gx'), may hold values from -6 to 6
- probe: float32 [2, 256, 256], replicated, may hold values from -6 to 6
- intensity: float32 [2048, 256, 256], P(('gx', 'gy')), may hold values from 0.1 to 4
- dest: int32 [2048, 1], P(('gx', 'gy')), may hold values from 0 to 15; in each aligned block of 16 rows (0 to 15, 16 to 31, ...) at most 2 rows name the same one
- offsets: int32 [2048, 2], P(('gx', 'gy')), may hold values from 0 to 511
Outputs:
- new_obj: float32 [2, 4096, 8192], P(None, 'gy', 'gx')
Inputs may be any that keep to these rules, and one draw needn't show every extreme that they name: `dest`: in each aligned block of 16 rows (the frames of one device) no tile column is named by more than 2 rows.
All inputs are finite; a program needn't handle non-finite values.
Results may differ from a plain program's by a relative error of at most 0.006.
Values may be sent and summed in bfloat16 or wider, within the bound.
No kernel may reach another device: no remote copies, remote signals or barrier semaphores. Data moves between devices by JAX's collectives and lax.ppermute only.
A program may use at most 192 MiB of HBM per device.

v0:
```python
import math

import jax
import jax.numpy as jnp
import numpy as np
from jax import lax
from jax.experimental import pallas as pl
from jax.experimental.pallas import tpu as pltpu
from jax.sharding import PartitionSpec as P

CAP = 2
FRAME = 256
HALF = 128
TILE = 512
EXTENT = TILE + 2 * HALF
PANELS = EXTENT // 128
BF16 = jnp.bfloat16
F32 = jnp.float32


def table_blocks():
    index = np.arange(FRAME)[:, None] * np.arange(FRAME)[None, :] % FRAME
    angle = index.astype(np.float32) * np.float32(2.0 * math.pi / FRAME)
    scale = np.float32(1.0 / math.sqrt(FRAME))
    re = (np.cos(angle) * scale).astype(BF16)
    im = (-np.sin(angle) * scale).astype(BF16)
    blocks = []
    for parity in (0, 1):
        c = re[:HALF, parity::2]
        s = im[:HALF, parity::2]
        fwd_right = np.block([[c, s], [-s, c]])
        fwd_left = fwd_right.T
        inv_right = np.block([[c.T, -s.T], [s.T, c.T]])
        inv_left = inv_right.T
        blocks.append([fwd_right, fwd_left, inv_right, inv_left])
    return np.stack([blocks[p][i] for i in range(4) for p in (0, 1)]).astype(BF16)


def deinterleave():
    perm = np.zeros((FRAME, FRAME), np.float32)
    for j in range(HALF):
        perm[2 * j, j] = 1.0
        perm[2 * j + 1, HALF + j] = 1.0
    return np.stack([perm, perm.T]).astype(BF16)


def dot(a, b):
    return jnp.dot(a, b, preferred_element_type=F32)


def prep_kernel(dest_ref, inten_ref, perm_ref, first_ref, second_ref, stage, sems):
    f = pl.program_id(0)
    count = pl.num_programs(0)
    slot = f % 2

    def wait_slot(s):
        pltpu.make_async_copy(stage.at[s], first_ref.at[0], sems.at[s]).wait()

    @pl.when(f >= 2)
    def _():
        wait_slot(slot)

    amp = jnp.sqrt(inten_ref[0]).astype(BF16)
    cols = dot(amp, perm_ref[0]).astype(BF16)
    stage[slot] = dot(perm_ref[1], cols).astype(BF16)
    mine = dest_ref[f]

    def count_same(i, total):
        return total + jnp.where(dest_ref[i] == mine, 1, 0)

    rank = lax.fori_loop(0, f, count_same, 0)

    @pl.when(rank == 0)
    def _():
        pltpu.make_async_copy(stage.at[slot], first_ref.at[mine], sems.at[slot]).start()

    @pl.when(rank != 0)
    def _():
        pltpu.make_async_copy(stage.at[slot], second_ref.at[mine], sems.at[slot]).start()

    @pl.when(f == count - 1)
    def _():
        wait_slot(slot)
        wait_slot(1 - slot)


def prep(dest, intensity, groups):
    frames = intensity.shape[0]
    out = jax.ShapeDtypeStruct((groups, FRAME, FRAME), BF16)
    return pl.pallas_call(
        prep_kernel,
        grid_spec=pltpu.PrefetchScalarGridSpec(
            num_scalar_prefetch=1,
            grid=(frames,),
            in_specs=[
                pl.BlockSpec((1, FRAME, FRAME), lambda f, d: (f, 0, 0)),
                pl.BlockSpec((2, FRAME, FRAME), lambda f, d: (0, 0, 0)),
            ],
            out_specs=[pl.BlockSpec(memory_space=pl.ANY)] * 2,
            scratch_shapes=[
                pltpu.VMEM((2, FRAME, FRAME), BF16),
                pltpu.SemaphoreType.DMA((2,)),
            ],
        ),
        out_shape=[out, out],
        compiler_params=pltpu.CompilerParams(vmem_limit_bytes=16 << 20),
        cost_estimate=pl.CostEstimate(
            flops=frames * 4 * FRAME**3, bytes_accessed=frames * FRAME * FRAME * 6, transcendentals=0
        ),
        name="prep",
    )(dest, intensity, jnp.asarray(deinterleave()))


def assemble_kernel(obj_ref, north_ref, south_ref, west_ref, east_ref, ext_ref):
    for part in range(2):
        ext_ref[part, 0] = west_ref[part].astype(F32)
        ext_ref[part, PANELS - 1] = east_ref[part].astype(F32)
        for j in range(TILE // 128):
            lanes = slice(128 * j, 128 * j + 128)
            ext_ref[part, j + 1, 0:HALF, :] = north_ref[part, :, lanes].astype(F32)
            ext_ref[part, j + 1, HALF : HALF + TILE, :] = obj_ref[part, :, lanes]
            ext_ref[part, j + 1, HALF + TILE :, :] = south_ref[part, :, lanes].astype(F32)


def assemble(obj, north, south, west, east):
    return pl.pallas_call(
        assemble_kernel,
        out_shape=jax.ShapeDtypeStruct((2, PANELS, EXTENT, 128), F32),
        compiler_params=pltpu.CompilerParams(vmem_limit_bytes=24 << 20),
        cost_estimate=pl.CostEstimate(flops=0, bytes_accessed=8 << 20, transcendentals=0),
        name="assemble",
    )(obj, north, south, west, east)


def process(row, col, amp, probe_ref, table_ref, ext_ref, acc_ref, xs, gs, ds, ms):
    panel = col // 128
    shift = col % 128
    back_shift = (128 - shift) % 128
    lane = lax.broadcasted_iota(jnp.int32, (FRAME, 128), 1)
    keep = lane < 128 - shift

    def cut(part):
        rolled = [
            pltpu.roll(ext_ref[part, panel + i, pl.ds(row, FRAME), :], back_shift, 1)
            for i in range(3)
        ]
        return [jnp.where(keep, rolled[i], rolled[i + 1]) for i in range(2)]

    patch_re = cut(0)
    patch_im = cut(1)
    ex_re, ex_im = [], []
    for h in range(2):
        lanes = slice(128 * h, 128 * h + 128)
        pr = probe_ref[0, :, lanes]
        pi = probe_ref[1, :, lanes]
        ex_re.append(pr * patch_re[h] - pi * patch_im[h])
        ex_im.append(pr * patch_im[h] + pi * patch_re[h])
    xs[0, :, 0:128] = (ex_re[0] + ex_re[1]).astype(BF16)
    xs[0, :, 128:256] = (ex_im[0] + ex_im[1]).astype(BF16)
    xs[1, :, 0:128] = (ex_re[0] - ex_re[1]).astype(BF16)
    xs[1, :, 128:256] = (ex_im[0] - ex_im[1]).astype(BF16)
    for q in range(2):
        half = dot(xs[q], table_ref[q])
        top, bottom = half[:HALF], half[HALF:]
        lanes = slice(128 * q, 128 * q + 128)
        for p, fold in ((0, top + bottom), (1, top - bottom)):
            folded = fold.astype(BF16)
            gs[p, 0:HALF, lanes] = folded[:, :128]
            gs[p, HALF:, lanes] = folded[:, 128:]
    for p in range(2):
        far = dot(table_ref[2 + p], gs[p])
        far_re, far_im = far[:HALF], far[HALF:]
        rows = slice(HALF * p, HALF * p + HALF)
        a = amp[rows].astype(F32)
        factor = a * lax.rsqrt(far_re * far_re + far_im * far_im + 1.0) - 1.0
        diff_re = (far_re * factor).astype(BF16)
        diff_im = (far_im * factor).astype(BF16)
        for q in range(2):
            lanes = slice(128 * q, 128 * q + 128)
            ds[q, rows, 0:128] = diff_re[:, lanes]
            ds[q, rows, 128:256] = diff_im[:, lanes]
    even = dot(ds[0], table_ref[4])
    odd = dot(ds[1], table_ref[5])
    for h, mid in ((0, (even + odd).astype(BF16)), (1, (even - odd).astype(BF16))):
        lanes = slice(128 * h, 128 * h + 128)
        for p in range(2):
            rows = slice(HALF * p, HALF * p + HALF)
            ms[p, 0:HALF, lanes] = mid[rows, :128]
            ms[p, HALF:, lanes] = mid[rows, 128:]
    even = dot(table_ref[6], ms[0])
    odd = dot(table_ref[7], ms[1])
    keep = lane[:HALF] < shift
    for v in range(2):
        back = even + odd if v == 0 else even - odd
        back_re, back_im = back[:HALF], back[HALF:]
        rows = slice(HALF * v, HALF * v + HALF)
        pr = probe_ref[0, rows]
        pi = probe_ref[1, rows]
        where = pl.ds(row + HALF * v, HALF)
        for part, term in ((0, pr * back_re + pi * back_im), (1, pr * back_im - pi * back_re)):
            left = pltpu.roll(term[:, :128], shift, 1)
            right = pltpu.roll(term[:, 128:], shift, 1)
            acc_ref[part, panel, where, :] += jnp.where(keep, 0.0, left)
            acc_ref[part, panel + 1, where, :] += jnp.where(keep, left, right)
            acc_ref[part, panel + 2, where, :] += jnp.where(keep, right, 0.0)


def first_kernel(meta_ref, amp_ref, probe_ref, table_ref, ext_ref, acc_ref, xs, gs, ds, ms):
    slot = pl.program_id(0)

    @pl.when(slot == 0)
    def _():
        acc_ref[...] = jnp.zeros_like(acc_ref)

    @pl.when(meta_ref[2, slot] > 0)
    def _():
        process(
            meta_ref[0, slot], meta_ref[1, slot], amp_ref.at[0][...], probe_ref, table_ref,
            ext_ref, acc_ref, xs, gs, ds, ms,
        )


def last_kernel(
    meta_ref, amp_ref, probe_ref, table_ref, ext_ref, start_ref,
    west_ref, east_ref, mid_ref, acc_ref, xs, gs, ds, ms,
):
    slot = pl.program_id(0)

    @pl.when(slot == 0)
    def _():
        acc_ref[...] = start_ref[...]

    @pl.when(meta_ref[2, slot] > 0)
    def _():
        process(
            meta_ref[0, slot], meta_ref[1, slot], amp_ref.at[0][...], probe_ref, table_ref,
            ext_ref, acc_ref, xs, gs, ds, ms,
        )

    @pl.when(slot == pl.num_programs(0) - 1)
    def _():
        for part in range(2):
            west_ref[part] = (0.5 * acc_ref[part, 0]).astype(BF16)
            east_ref[part] = (0.5 * acc_ref[part, PANELS - 1]).astype(BF16)
            for j in range(TILE // 128):
                lanes = slice(128 * j, 128 * j + 128)
                inner = slice(HALF, HALF + TILE)
                mid_ref[part, 0:HALF, lanes] = 0.5 * acc_ref[part, j + 1, 0:HALF, :]
                mid_ref[part, inner, lanes] = (
                    ext_ref[part, j + 1, inner, :] + 0.5 * acc_ref[part, j + 1, inner, :]
                )
                mid_ref[part, HALF + TILE :, lanes] = 0.5 * acc_ref[part, j + 1, HALF + TILE :, :]


def whole(shape):
    return pl.BlockSpec(shape, lambda s, m: (0,) * len(shape))


def run_slots(meta, amps, probe, tabs, ext, acc=None):
    slots = amps.shape[0]
    wide = (2, PANELS, EXTENT, 128)
    in_specs = [
        pl.BlockSpec((1, FRAME, FRAME), lambda s, m: (s, 0, 0)),
        whole((2, FRAME, FRAME)),
        whole((8, FRAME, FRAME)),
        whole(wide),
    ]
    operands = [meta, amps, probe, tabs, ext]
    scratch = [pltpu.VMEM((2, FRAME, FRAME), BF16) for _ in range(4)]
    if acc is None:
        kernel = first_kernel
        out_shape = jax.ShapeDtypeStruct(wide, F32)
        out_specs = whole(wide)
    else:
        kernel = last_kernel
        in_specs.append(whole(wide))
        operands.append(acc)
        shapes = [(2, EXTENT, 128), (2, EXTENT, 128), (2, EXTENT, TILE)]
        out_shape = [jax.ShapeDtypeStruct(s, d) for s, d in zip(shapes, (BF16, BF16, F32))]
        out_specs = [whole(s) for s in shapes]
        scratch = [pltpu.VMEM(wide, F32)] + scratch
    return pl.pallas_call(
        kernel,
        grid_spec=pltpu.PrefetchScalarGridSpec(
            num_scalar_prefetch=1,
            grid=(slots,),
            in_specs=in_specs,
            out_specs=out_specs,
            scratch_shapes=scratch,
        ),
        out_shape=out_shape,
        compiler_params=pltpu.CompilerParams(vmem_limit_bytes=56 << 20),
        cost_estimate=pl.CostEstimate(
            flops=slots * 16 * FRAME**3, bytes_accessed=16 << 20, transcendentals=0
        ),
        name="slots",
    )(*operands)


def finish_kernel(base_ref, strip_ref, out_ref):
    out_ref[...] = base_ref[...] + strip_ref[0].astype(F32)


def shifted(value, axis, by):
    size = lax.axis_size(axis)
    pairs = [(i, i + by) for i in range(size) if 0 <= i + by < size]
    return lax.ppermute(value, axis, pairs)


def body(obj, probe, intensity, dest, offsets):
    groups = lax.axis_size("gx")
    frames = intensity.shape[0]
    me = lax.axis_index("gx")
    info = lax.all_gather(jnp.concatenate([dest, offsets], axis=1), "gx", axis=0)
    hit = info[:, :, 0] == me
    order = jnp.cumsum(hit.astype(jnp.int32), axis=1)
    metas = []
    for rank in range(CAP):
        pick = (hit & (order == rank + 1)).astype(jnp.int32)
        metas.append(
            jnp.stack(
                [
                    jnp.sum(pick * info[:, :, 1], axis=1),
                    jnp.sum(pick * info[:, :, 2], axis=1),
                    jnp.sum(pick, axis=1),
                ]
            )
        )
    sends = prep(dest[:, 0], intensity, groups)
    north = shifted(obj[:, TILE - HALF :, :].astype(BF16), "gy", 1)
    south = shifted(obj[:, :HALF, :].astype(BF16), "gy", -1)
    amps = [lax.all_to_all(s, "gx", split_axis=0, concat_axis=0, tiled=True) for s in sends]

    def column(lo, hi):
        own = obj[:, :, lo:hi].astype(BF16)
        return jnp.concatenate([north[:, :, lo:hi], own, south[:, :, lo:hi]], axis=1)

    west = shifted(column(TILE - HALF, TILE), "gx", 1)
    east = shifted(column(0, HALF), "gx", -1)
    ext = assemble(obj, north, south, west, east)
    tabs = jnp.asarray(table_blocks())
    acc = run_slots(metas[0], amps[0], probe, tabs, ext)
    west, east, mid = run_slots(metas[1], amps[1], probe, tabs, ext, acc)
    from_west = shifted(east, "gx", 1).astype(F32)
    from_east = shifted(west, "gx", -1).astype(F32)

    def summed(lo, hi):
        rows = mid[:, lo:hi]
        left = rows[:, :, :HALF] + from_west[:, lo:hi]
        right = rows[:, :, TILE - HALF :] + from_east[:, lo:hi]
        return jnp.concatenate([left, rows[:, :, HALF : TILE - HALF], right], axis=2)

    to_north = summed(0, HALF).astype(BF16)
    to_south = summed(HALF + TILE, EXTENT).astype(BF16)
    from_north = shifted(to_south, "gy", 1)
    from_south = shifted(to_north, "gy", -1)
    inner = summed(HALF, HALF + TILE)
    strips = jnp.stack([from_north, from_south])
    return pl.pallas_call(
        finish_kernel,
        grid=(2,),
        in_specs=[
            pl.BlockSpec((2, HALF, TILE), lambda i: (0, 3 * i, 0)),
            pl.BlockSpec((1, 2, HALF, TILE), lambda i: (i, 0, 0, 0)),
        ],
        out_specs=pl.BlockSpec((2, HALF, TILE), lambda i: (0, 3 * i, 0)),
        out_shape=jax.ShapeDtypeStruct((2, TILE, TILE), F32),
        input_output_aliases={0: 0},
        name="finish",
    )(inner, strips)


def solution(mesh):
    placed = (
        P(None, "gy", "gx"),
        P(),
        P(("gx", "gy"), None, None),
        P(("gx", "gy"), None),
        P(("gx", "gy"), None),
    )
    return jax.shard_map(
        body, mesh=mesh, in_specs=placed, out_specs=P(None, "gy", "gx"), check_vma=False
    )
```

profile of v0, /device:TPU:120, one launch (start us, length us, event | category | flops | bytes accessed | tf_op | source)
XLA Modules:
  0.0 205.2 jit_solution(7621652663318635642)
XLA Ops:
  0.0 2.2 %copy-done.2 = f32[16,256,256]{2,1,0:T(8,128)S(1)} copy-done((f32[16,256,256]{2,1,0:T(8,128)S(1)}, f32[16,256,256]{2,1,0:T(8,128)}, u32[]{:S(2)}) %copy-start.2) | copy-done | bytes 4194328
  2.2 0.9 copy-done.5
  3.1 0.7 copy-done.6
  3.8 10.7 %prep.1 = (bf16[16,256,256]{2,1,0:T(8,128)(2,1)S(1)}, bf16[16,256,256]{2,1,0:T(8,128)(2,1)S(1)}) custom-call(s32[16]{0:T(128)S(1)} %bitcast.22, f32[16,256,256]{2,1,0:T(8,128)S(1)} %copy-done.2, bf16[2,256,256]{2,1,0:T(8,128)(2,1)S(1)} %copy-done.5), custom_call_target="tpu_custom_call" | custom-call | flops 1073741824 | bytes 6291456 | tf_op jit(solution)/shard_map/prep/pallas_call | solution.py:90
  14.5 0.0 copy-start.3
  14.5 1.3 copy-done.3
  15.8 1.3 copy-done.4
  17.2 7.3 %all-to-all-start.1 = ((bf16[16,256,256]{2,1,0:T(8,128)(2,1)}), bf16[16,256,256]{2,1,0:T(8,128)(2,1)}, u32[]{:S(2)}, u32[]{:S(2)}) async-start(bf16[16,256,256]{2,1,0:T(8,128)(2,1)} %copy-done.4), calls=%async_computation.1 | async-start | bytes 4194304 | tf_op jit(solution)/shard_map/all_to_all | solution.py:332
  24.5 0.0 copy-start.7
  24.5 0.0 copy-start.9
  24.5 0.1 convert.24
  24.6 0.7 fusion.6
  25.4 2.3 %collective-permute-start.1 = (bf16[2,128,512]{2,1,0:T(8,128)(2,1)}, bf16[2,128,512]{2,1,0:T(8,128)(2,1)S(1)}, u32[]{:S(2)}, u32[]{:S(2)}) collective-permute-start(bf16[2,128,512]{2,1,0:T(8,128)(2,1)} %get-tuple-element.37), channel_id=1, source_target_pairs={{1,0},{2,1},{3,2},{4,3},{5,4},{6,5},{7,6},{9,8},{10,9},{11,10},{12... | collective-permute-start | bytes 786440 | tf_op jit(solution)/shard_map/ppermute | solution.py:307
  27.7 3.5 %collective-permute-start = (bf16[2,128,512]{2,1,0:T(8,128)(2,1)S(1)}, bf16[2,128,512]{2,1,0:T(8,128)(2,1)S(1)}, u32[]{:S(2)}, u32[]{:S(2)}) collective-permute-start(bf16[2,128,512]{2,1,0:T(8,128)(2,1)S(1)} %get-tuple-element.38), channel_id=1, source_target_pairs={{0,1},{1,2},{2,3},{3,4},{4,5},{5,6},{6,7},{8,9},{9,10},{10,11},{11... | collective-permute-start | bytes 786440 | tf_op jit(solution)/shard_map/ppermute | solution.py:307
  31.3 42.9 %all-gather.1 = s32[16,16,3]{1,2,0:T(4,128)S(1)} all-gather(s32[1,16,3]{1,2,0:T(4,128)S(1)} %add_bitcast_fusion), channel_id=2, replica_groups=mesh['gx'=16,'gy'=8] {'gx'}, dimensions={0}, use_global_device_ids=true | all-gather | bytes 3264 | tf_op jit(solution)/shard_map/all_gather | solution.py:314
  74.2 0.1 fusion.5
  74.3 0.0 all-to-all-done.1.amp_ref
  74.3 8.0 %all-to-all-start = ((bf16[16,256,256]{2,1,0:T(8,128)(2,1)}), bf16[16,256,256]{2,1,0:T(8,128)(2,1)}, u32[]{:S(2)}, u32[]{:S(2)}) async-start(bf16[16,256,256]{2,1,0:T(8,128)(2,1)} %copy-done.3), calls=%async_computation | async-start | bytes 4194304 | tf_op jit(solution)/shard_map/all_to_all | solution.py:332
  82.4 0.2 reduce_window_sum.11
  82.6 0.0 collective-permute-done.1.south_ref
  82.6 0.0 collective-permute-done.north_ref
  82.7 2.1 %collective-permute-start.2 = (bf16[2,768,128]{2,1,0:T(8,128)(2,1)S(1)}, bf16[2,768,128]{2,1,0:T(8,128)(2,1)S(1)}, u32[]{:S(2)}, u32[]{:S(2)}) collective-permute-start(bf16[2,768,128]{2,1,0:T(8,128)(2,1)S(1)} %pad_maximum_fusion.2), channel_id=1, source_target_pairs={{0,8},{8,16},{16,24},{24,32},{32,40},{40,48},{48,56},{56,64},{64,7... | collective-permute-start | bytes 1179656 | tf_op jit(solution)/shard_map/ppermute | solution.py:307
  84.8 5.9 %collective-permute-start.3 = (bf16[2,768,128]{2,1,0:T(8,128)(2,1)S(1)}, bf16[2,768,128]{2,1,0:T(8,128)(2,1)S(1)}, u32[]{:S(2)}, u32[]{:S(2)}) collective-permute-start(bf16[2,768,128]{2,1,0:T(8,128)(2,1)S(1)} %pad_maximum_fusion.3), channel_id=1, source_target_pairs={{8,0},{16,8},{24,16},{32,24},{40,32},{48,40},{56,48},{64,56},{72,6... | collective-permute-start | bytes 1179656 | tf_op jit(solution)/shard_map/ppermute | solution.py:307
  90.7 0.2 select_reduce_fusion
  90.9 0.6 pad_add_fusion.meta_ref
  91.5 0.6 pad_add_fusion.1.meta_ref
  92.1 25.3 %collective-permute-done.2.west_ref = bf16[2,768,128]{2,1,0:T(8,128)(2,1)S(1)} collective-permute-done((bf16[2,768,128]{2,1,0:T(8,128)(2,1)S(1)}, bf16[2,768,128]{2,1,0:T(8,128)(2,1)S(1)}, u32[]{:S(2)}, u32[]{:S(2)}) %collective-permute-start.2) | collective-permute-done | bytes 393248 | tf_op jit(solution)/shard_map/ppermute | solution.py:307
  117.4 0.0 collective-permute-done.3.east_ref
  117.4 0.3 assemble.1.ext_ref
  117.7 2.1 %copy-done.1 = f32[2,6,768,128]{3,2,1,0:T(8,128)} copy-done((f32[2,6,768,128]{3,2,1,0:T(8,128)}, f32[2,6,768,128]{3,2,1,0:T(8,128)S(1)}, u32[]{:S(2)}) %copy-start.1) | copy-done | bytes 4718616
  119.8 26.9 %slots.2.start_ref = f32[2,6,768,128]{3,2,1,0:T(8,128)} custom-call(s32[3,16]{1,0:T(4,128)} %pad_add_fusion.1.meta_ref, bf16[16,256,256]{2,1,0:T(8,128)(2,1)} %all-to-all-done.1.amp_ref, f32[2,256,256]{2,1,0:T(8,128)} %probe_ref.3, bf16[8,256,256]{2,1,0:T(8,128)(2,1)} %constant.24.clone.table_ref, f32[2,6,768,128]{3,2,1,0:T(8,128)} %copy-done.1), custom_call_target="tpu_custom_call" | custom-call | flops 4294967296 | bytes 16777216 | tf_op jit(solution)/shard_map/slots/pallas_call | solution.py:282
  146.7 14.2 %slots.3 = (bf16[2,768,128]{2,1,0:T(8,128)(2,1)}, bf16[2,768,128]{2,1,0:T(8,128)(2,1)}, f32[2,768,512]{2,1,0:T(8,128)}) custom-call(s32[3,16]{1,0:T(4,128)} %pad_add_fusion.meta_ref, bf16[16,256,256]{2,1,0:T(8,128)(2,1)} %all-to-all-done.amp_ref, f32[2,256,256]{2,1,0:T(8,128)} %probe_ref.3, bf16[8,256,256]{2,1,0:T(8,128)(2,1)} %constant.24.clone.table_ref, ...), custom_call_target="tpu_custom_call" | custom-call | flops 4294967296 | bytes 16777216 | tf_op jit(solution)/shard_map/slots/pallas_call | solution.py:282
  160.9 16.1 %collective-permute-start.4 = (bf16[2,768,128]{2,1,0:T(8,128)(2,1)}, bf16[2,768,128]{2,1,0:T(8,128)(2,1)S(1)}, u32[]{:S(2)}, u32[]{:S(2)}) collective-permute-start(bf16[2,768,128]{2,1,0:T(8,128)(2,1)} %get-tuple-element.13), channel_id=1, source_target_pairs={{0,8},{8,16},{16,24},{24,32},{32,40},{40,48},{48,56},{56,64},{64,7... | collective-permute-start | bytes 1179656 | tf_op jit(solution)/shard_map/ppermute | solution.py:307
  177.0 1.9 collective-permute-start.5
  178.9 1.3 slice.111
  180.3 2.2 %convert.26 = bf16[2,768,512]{2,1,0:T(8,128)(2,1)S(1)} convert(f32[2,768,512]{2,1,0:T(8,128)} %get-tuple-element.12) | non-fusion elementwise | flops 786432 | bytes 4718592 | tf_op jit(solution)/shard_map/convert.7
  182.5 0.1 convert_element_type.24
  182.6 3.5 %collective-permute-done.5 = bf16[2,768,128]{2,1,0:T(8,128)(2,1)S(1)} collective-permute-done((bf16[2,768,128]{2,1,0:T(8,128)(2,1)}, bf16[2,768,128]{2,1,0:T(8,128)(2,1)S(1)}, u32[]{:S(2)}, u32[]{:S(2)}) %collective-permute-start.5) | collective-permute-done | bytes 393248 | tf_op jit(solution)/shard_map/ppermute | solution.py:307
  186.1 0.1 convert_element_type.25
  186.2 0.1 fusion.3
  186.3 1.9 collective-permute-start.7
  188.3 3.9 %collective-permute-start.6 = (bf16[2,128,512]{2,1,0:T(8,128)(2,1)S(1)}, bf16[2,128,512]{2,1,0:T(8,128)(2,1)S(1)}, u32[]{:S(2)}, u32[]{:S(2)}) collective-permute-start(bf16[2,128,512]{2,1,0:T(8,128)(2,1)S(1)} %pad_maximum_fusion.4), channel_id=1, source_target_pairs={{0,1},{1,2},{2,3},{3,4},{4,5},{5,6},{6,7},{8,9},{9,10},{10,11},{11... | collective-permute-start | bytes 786440 | tf_op jit(solution)/shard_map/ppermute | solution.py:307
  192.2 0.1 slice_add_fusion.1
  192.4 1.5 pad_maximum_fusion.base_ref
  193.9 2.8 %collective-permute-done.7 = bf16[2,128,512]{2,1,0:T(8,128)(2,1)S(1)} collective-permute-done((bf16[2,128,512]{2,1,0:T(8,128)(2,1)S(1)}, bf16[2,128,512]{2,1,0:T(8,128)(2,1)S(1)}, u32[]{:S(2)}, u32[]{:S(2)}) %collective-permute-start.7) | collective-permute-done | bytes 262176 | tf_op jit(solution)/shard_map/ppermute | solution.py:307
  196.7 5.5 %collective-permute-done.6 = bf16[2,128,512]{2,1,0:T(8,128)(2,1)S(1)} collective-permute-done((bf16[2,128,512]{2,1,0:T(8,128)(2,1)S(1)}, bf16[2,128,512]{2,1,0:T(8,128)(2,1)S(1)}, u32[]{:S(2)}, u32[]{:S(2)}) %collective-permute-start.6) | collective-permute-done | bytes 262176 | tf_op jit(solution)/shard_map/ppermute | solution.py:307
  202.2 0.8 pad_maximum_fusion.1.strip_ref
  203.0 2.2 %finish.1 = f32[2,512,512]{2,1,0:T(8,128)} custom-call(f32[2,512,512]{2,1,0:T(8,128)} %pad_maximum_fusion.base_ref, bf16[2,2,128,512]{3,2,1,0:T(8,128)(2,1)} %pad_maximum_fusion.1.strip_ref), custom_call_target="tpu_custom_call", output_to_operand_aliasing={{}: (0, {})} | custom-call | tf_op jit(solution)/shard_map/finish/pallas_call | solution.py:359
  (24 shorter events, 0.3 us)
Async XLA Ops:
  0.0 2.2 %copy-start.2 = (f32[16,256,256]{2,1,0:T(8,128)S(1)}, f32[16,256,256]{2,1,0:T(8,128)}, u32[]{:S(2)}) copy-start(f32[16,256,256]{2,1,0:T(8,128)} %inten_ref.1) | copy-start | bytes 12582916
  2.2 0.9 copy-start.5
  3.1 0.7 copy-start.6
  14.5 1.3 copy-start.3
  15.8 1.3 copy-start.4
  17.2 7.3 %copy-start = (f32[2,512,512]{2,1,0:T(8,128)S(1)}, f32[2,512,512]{2,1,0:T(8,128)}, u32[]{:S(2)}) copy-start(f32[2,512,512]{2,1,0:T(8,128)} %obj_ref.1) | copy-start | bytes 6291460
  17.2 57.1 %all-to-all-start.1 = ((bf16[16,256,256]{2,1,0:T(8,128)(2,1)}), bf16[16,256,256]{2,1,0:T(8,128)(2,1)}, u32[]{:S(2)}, u32[]{:S(2)}) async-start(bf16[16,256,256]{2,1,0:T(8,128)(2,1)} %copy-done.4), calls=%async_computation.1 | async-start | bytes 4194304 | tf_op jit(solution)/shard_map/all_to_all | solution.py:332
  24.5 6.8 %copy-start.7 = (s32[16,1]{0,1:T(1,128)S(1)}, s32[16,1]{0,1:T(1,128)}, u32[]{:S(2)}) copy-start(s32[16,1]{0,1:T(1,128)} %param.10) | copy-start | bytes 196
  24.5 6.8 %copy-start.9 = (s32[16,2]{0,1:T(2,128)S(1)}, s32[16,2]{0,1:T(2,128)}, u32[]{:S(2)}) copy-start(s32[16,2]{0,1:T(2,128)} %param.11) | copy-start | bytes 388
  25.4 57.2 %collective-permute-start.1 = (bf16[2,128,512]{2,1,0:T(8,128)(2,1)}, bf16[2,128,512]{2,1,0:T(8,128)(2,1)S(1)}, u32[]{:S(2)}, u32[]{:S(2)}) collective-permute-start(bf16[2,128,512]{2,1,0:T(8,128)(2,1)} %get-tuple-element.37), channel_id=1, source_target_pairs={{1,0},{2,1},{3,2},{4,3},{5,4},{6,5},{7,6},{9,8},{10,9},{11,10},{12... | collective-permute-start | bytes 786440 | tf_op jit(solution)/shard_map/ppermute | solution.py:307
  27.7 54.9 %collective-permute-start = (bf16[2,128,512]{2,1,0:T(8,128)(2,1)S(1)}, bf16[2,128,512]{2,1,0:T(8,128)(2,1)S(1)}, u32[]{:S(2)}, u32[]{:S(2)}) collective-permute-start(bf16[2,128,512]{2,1,0:T(8,128)(2,1)S(1)} %get-tuple-element.38), channel_id=1, source_target_pairs={{0,1},{1,2},{2,3},{3,4},{4,5},{5,6},{6,7},{8,9},{9,10},{10,11},{11... | collective-permute-start | bytes 786440 | tf_op jit(solution)/shard_map/ppermute | solution.py:307
  74.3 72.4 %all-to-all-start = ((bf16[16,256,256]{2,1,0:T(8,128)(2,1)}), bf16[16,256,256]{2,1,0:T(8,128)(2,1)}, u32[]{:S(2)}, u32[]{:S(2)}) async-start(bf16[16,256,256]{2,1,0:T(8,128)(2,1)} %copy-done.3), calls=%async_computation | async-start | bytes 4194304 | tf_op jit(solution)/shard_map/all_to_all | solution.py:332
  82.7 34.7 %collective-permute-start.2 = (bf16[2,768,128]{2,1,0:T(8,128)(2,1)S(1)}, bf16[2,768,128]{2,1,0:T(8,128)(2,1)S(1)}, u32[]{:S(2)}, u32[]{:S(2)}) collective-permute-start(bf16[2,768,128]{2,1,0:T(8,128)(2,1)S(1)} %pad_maximum_fusion.2), channel_id=1, source_target_pairs={{0,8},{8,16},{16,24},{24,32},{32,40},{40,48},{48,56},{56,64},{64,7... | collective-permute-start | bytes 1179656 | tf_op jit(solution)/shard_map/ppermute | solution.py:307
  84.8 32.6 %collective-permute-start.3 = (bf16[2,768,128]{2,1,0:T(8,128)(2,1)S(1)}, bf16[2,768,128]{2,1,0:T(8,128)(2,1)S(1)}, u32[]{:S(2)}, u32[]{:S(2)}) collective-permute-start(bf16[2,768,128]{2,1,0:T(8,128)(2,1)S(1)} %pad_maximum_fusion.3), channel_id=1, source_target_pairs={{8,0},{16,8},{24,16},{32,24},{40,32},{48,40},{56,48},{64,56},{72,6... | collective-permute-start | bytes 1179656 | tf_op jit(solution)/shard_map/ppermute | solution.py:307
  117.7 2.1 %copy-start.1 = (f32[2,6,768,128]{3,2,1,0:T(8,128)}, f32[2,6,768,128]{3,2,1,0:T(8,128)S(1)}, u32[]{:S(2)}) copy-start(f32[2,6,768,128]{3,2,1,0:T(8,128)S(1)} %assemble.1.ext_ref) | copy-start | bytes 14155780
  160.9 21.6 %collective-permute-start.4 = (bf16[2,768,128]{2,1,0:T(8,128)(2,1)}, bf16[2,768,128]{2,1,0:T(8,128)(2,1)S(1)}, u32[]{:S(2)}, u32[]{:S(2)}) collective-permute-start(bf16[2,768,128]{2,1,0:T(8,128)(2,1)} %get-tuple-element.13), channel_id=1, source_target_pairs={{0,8},{8,16},{16,24},{24,32},{32,40},{40,48},{48,56},{56,64},{64,7... | collective-permute-start | bytes 1179656 | tf_op jit(solution)/shard_map/ppermute | solution.py:307
  177.0 9.1 %collective-permute-start.5 = (bf16[2,768,128]{2,1,0:T(8,128)(2,1)}, bf16[2,768,128]{2,1,0:T(8,128)(2,1)S(1)}, u32[]{:S(2)}, u32[]{:S(2)}) collective-permute-start(bf16[2,768,128]{2,1,0:T(8,128)(2,1)} %get-tuple-element.14), channel_id=1, source_target_pairs={{8,0},{16,8},{24,16},{32,24},{40,32},{48,40},{56,48},{64,56},{72,6... | collective-permute-start | bytes 1179656 | tf_op jit(solution)/shard_map/ppermute | solution.py:307
  180.2 5.9 %copy-start.8 = (f32[2,768,512]{2,1,0:T(8,128)S(1)}, f32[2,768,512]{2,1,0:T(8,128)}, u32[]{:S(2)}) copy-start(f32[2,768,512]{2,1,0:T(8,128)} %get-tuple-element.12) | copy-start | bytes 9437188
  186.3 10.4 %collective-permute-start.7 = (bf16[2,128,512]{2,1,0:T(8,128)(2,1)S(1)}, bf16[2,128,512]{2,1,0:T(8,128)(2,1)S(1)}, u32[]{:S(2)}, u32[]{:S(2)}) collective-permute-start(bf16[2,128,512]{2,1,0:T(8,128)(2,1)S(1)} %pad_maximum_fusion.5), channel_id=1, source_target_pairs={{1,0},{2,1},{3,2},{4,3},{5,4},{6,5},{7,6},{9,8},{10,9},{11,10},{12... | collective-permute-start | bytes 786440 | tf_op jit(solution)/shard_map/ppermute | solution.py:307
  188.3 13.9 %collective-permute-start.6 = (bf16[2,128,512]{2,1,0:T(8,128)(2,1)S(1)}, bf16[2,128,512]{2,1,0:T(8,128)(2,1)S(1)}, u32[]{:S(2)}, u32[]{:S(2)}) collective-permute-start(bf16[2,128,512]{2,1,0:T(8,128)(2,1)S(1)} %pad_maximum_fusion.4), channel_id=1, source_target_pairs={{0,1},{1,2},{2,3},{3,4},{4,5},{5,6},{6,7},{8,9},{9,10},{10,11},{11... | collective-permute-start | bytes 786440 | tf_op jit(solution)/shard_map/ppermute | solution.py:307
where the time goes:
time: 209 us; the launch traced here: 205 us
  Pallas kernels  54.3 us (26%)
  starting transfers between devices  53 us (25%)
  blocking collectives  42.9 us (21%)
  waiting for transfers between devices  37.1 us (18%)
  local copies, waits for them, and re-layouts  10.8 us (5%)
  other arithmetic  6.81 us (3%)
    all_gather x1, blocking collectives, body(): lax.all_gather(jnp.concatenate([dest, offsets], axis=1), 'gx', axis=0)  42.9 us
    pallas_call x2, Pallas kernels, run_slots(): pl.pallas_call(kernel, grid_spec=pltpu.PrefetchScalarGridSpec(num_scalar_...  41.1 us
    ppermute x8, starting transfers between devices, shifted(): return lax.ppermute(value, axis, pairs)  37.6 us
    ppermute x8, waiting for transfers between devices, shifted(): return lax.ppermute(value, axis, pairs)  37.1 us
    all_to_all x2, starting transfers between devices, body(): lax.all_to_all(s, 'gx', split_axis=0, concat_axis=0, tiled=True)  15.3 us
    pallas_call x1, Pallas kernels, prep(): pl.pallas_call(prep_kernel, grid_spec=pltpu.PrefetchScalarGridSpec(num_sc...  10.7 us
    unnamed x20, local copies, waits for them, and re-layouts  8.58 us
  transfers between devices with their start and end apart: 10, of which 4 were waited for; matrix products, arithmetic and copies ran while one was open for 4% of the time, Pallas kernels for 13%

commit v1 on v0

v1 whole, which is shorter than its diff:
```python
import math

import jax
import jax.numpy as jnp
import numpy as np
from jax import lax
from jax.experimental import pallas as pl
from jax.experimental.pallas import tpu as pltpu
from jax.sharding import PartitionSpec as P

CAP = 2
FRAME = 256
HALF = 128
TILE = 512
EXTENT = TILE + 2 * HALF
PANELS = EXTENT // 128
NOTE_ROWS = 16
GROUP = 4
BF16 = jnp.bfloat16
F32 = jnp.float32


def table_blocks():
    index = np.arange(FRAME)[:, None] * np.arange(FRAME)[None, :] % FRAME
    angle = index.astype(np.float32) * np.float32(2.0 * math.pi / FRAME)
    scale = np.float32(1.0 / math.sqrt(FRAME))
    re = (np.cos(angle) * scale).astype(BF16)
    im = (-np.sin(angle) * scale).astype(BF16)
    blocks = []
    for parity in (0, 1):
        c = re[:HALF, parity::2]
        s = im[:HALF, parity::2]
        fwd_right = np.block([[c, s], [-s, c]])
        fwd_left = fwd_right.T
        inv_right = np.block([[c.T, -s.T], [s.T, c.T]])
        inv_left = inv_right.T
        blocks.append([fwd_right, fwd_left, inv_right, inv_left])
    return np.stack([blocks[p][i] for i in range(4) for p in (0, 1)]).astype(BF16)


def deinterleave():
    perm = np.zeros((FRAME, FRAME), np.float32)
    for j in range(HALF):
        perm[2 * j, j] = 1.0
        perm[2 * j + 1, HALF + j] = 1.0
    return perm.astype(BF16)


def dot(a, b):
    return jnp.dot(a, b, preferred_element_type=F32)


def prep_kernel(dest_ref, offs_ref, left_ref, right_ref, perm_ref, first_ref, second_ref, stage, notes, ranks, sems):
    step = pl.program_id(0)
    count = pl.num_programs(0)
    per = left_ref.shape[0]
    groups = first_ref.shape[0]
    slot = step % 2

    def notes_copy():
        return pltpu.make_async_copy(
            notes, first_ref.at[:, pl.ds(2 * FRAME, NOTE_ROWS), :], sems.at[2 * per]
        )

    @pl.when(step == 0)
    def _():
        lane = lax.broadcasted_iota(jnp.int32, (1, 1, 128), 2)
        owner = lax.broadcasted_iota(jnp.int32, (groups, 1, 128), 0)
        lane = jnp.broadcast_to(lane, (groups, 1, 128))
        note = jnp.zeros((groups, 1, 128), jnp.int32)
        for g in range(groups):
            ranks[per * count + g] = 0
        for f in range(per * count):
            mine = dest_ref[f]
            rank = ranks[per * count + mine]
            ranks[f] = rank
            ranks[per * count + mine] = rank + 1
            row, col = offs_ref[2 * f], offs_ref[2 * f + 1]
            at = lane - 5 * rank
            value = jnp.where(at == 0, row // 16, jnp.where(at == 1, row % 16, 0))
            value += jnp.where(at == 2, col // 16, jnp.where(at == 3, col % 16, 0))
            value += jnp.where(at == 4, 1, 0)
            note = jnp.where(owner == mine, note + value, note)
        notes[...] = jnp.broadcast_to(note.astype(F32), notes.shape).astype(BF16)
        notes_copy().start()

    for i in range(per):

        @pl.when(step >= 2)
        def _():
            pltpu.make_async_copy(
                stage.at[slot, i], second_ref.at[0], sems.at[slot * per + i]
            ).wait()

    for i in range(per):
        rows = [
            jnp.concatenate([ref[i, pl.ds(p, HALF, 2), :] for ref in (left_ref, right_ref)], axis=1)
            for p in range(2)
        ]
        amp = jnp.sqrt(jnp.concatenate(rows, axis=0)).astype(BF16)
        cols = dot(amp, perm_ref[...]).astype(BF16)
        stage[slot, i, 0:FRAME, :] = cols[:, :128]
        stage[slot, i, FRAME : 2 * FRAME, :] = cols[:, 128:]
    for i in range(per):
        f = step * per + i
        mine = dest_ref[f]
        rank = ranks[f]

        @pl.when(rank == 0)
        def _():
            pltpu.make_async_copy(
                stage.at[slot, i],
                first_ref.at[mine, pl.ds(0, 2 * FRAME), :],
                sems.at[slot * per + i],
            ).start()

        @pl.when(rank != 0)
        def _():
            pltpu.make_async_copy(
                stage.at[slot, i], second_ref.at[mine], sems.at[slot * per + i]
            ).start()

    @pl.when(step == count - 1)
    def _():
        notes_copy().wait()
        for s in range(2):
            for i in range(per):
                pltpu.make_async_copy(
                    stage.at[s, i], second_ref.at[0], sems.at[s * per + i]
                ).wait()


def prep(dest, offsets, intensity, groups):
    frames = intensity.shape[0]
    per = 2
    return pl.pallas_call(
        prep_kernel,
        grid_spec=pltpu.PrefetchScalarGridSpec(
            num_scalar_prefetch=2,
            grid=(frames // per,),
            in_specs=[
                pl.BlockSpec((per, FRAME, 128), lambda s, d, o: (s, 0, 0)),
                pl.BlockSpec((per, FRAME, 128), lambda s, d, o: (s, 0, 1)),
                pl.BlockSpec((FRAME, FRAME), lambda s, d, o: (0, 0)),
            ],
            out_specs=[pl.BlockSpec(memory_space=pl.ANY)] * 2,
            scratch_shapes=[
                pltpu.VMEM((2, per, 2 * FRAME, 128), BF16),
                pltpu.VMEM((groups, NOTE_ROWS, 128), BF16),
                pltpu.SMEM((frames + groups,), jnp.int32),
                pltpu.SemaphoreType.DMA((2 * per + 1,)),
            ],
        ),
        out_shape=[
            jax.ShapeDtypeStruct((groups, 2 * FRAME + NOTE_ROWS, 128), BF16),
            jax.ShapeDtypeStruct((groups, 2 * FRAME, 128), BF16),
        ],
        compiler_params=pltpu.CompilerParams(vmem_limit_bytes=56 << 20),
        cost_estimate=pl.CostEstimate(
            flops=frames * 2 * FRAME**3, bytes_accessed=frames * FRAME * FRAME * 6, transcendentals=0
        ),
        name="prep",
    )(dest, offsets, intensity, intensity, jnp.asarray(deinterleave()))


def assemble_kernel(obj_ref, north_ref, south_ref, west_ref, east_ref, ext_ref):
    for part in range(2):
        ext_ref[part, 0] = west_ref[part].astype(F32)
        ext_ref[part, PANELS - 1] = east_ref[part].astype(F32)
        for j in range(TILE // 128):
            lanes = slice(128 * j, 128 * j + 128)
            ext_ref[part, j + 1, 0:HALF, :] = north_ref[part, :, lanes].astype(F32)
            ext_ref[part, j + 1, HALF : HALF + TILE, :] = obj_ref[part, :, lanes]
            ext_ref[part, j + 1, HALF + TILE :, :] = south_ref[part, :, lanes].astype(F32)


def assemble(obj, north, south, west, east):
    return pl.pallas_call(
        assemble_kernel,
        out_shape=jax.ShapeDtypeStruct((2, PANELS, EXTENT, 128), F32),
        compiler_params=pltpu.CompilerParams(vmem_limit_bytes=24 << 20),
        cost_estimate=pl.CostEstimate(flops=0, bytes_accessed=8 << 20, transcendentals=0),
        name="assemble",
    )(obj, north, south, west, east)


def process(places, amp_ref, probe_ref, table_ref, ext_ref, acc_ref, xs, gs, ds, ms):
    members = range(len(places))
    lane = lax.broadcasted_iota(jnp.int32, (FRAME, 128), 1)
    rows_of = [slice(FRAME * m, FRAME * m + FRAME) for m in members]
    for m in members:
        row, col, live = places[m]
        panel = col // 128
        shift = col % 128
        back_shift = (128 - shift) % 128
        keep = lane < 128 - shift

        def cut(part):
            rolled = [
                pltpu.roll(ext_ref[part, panel + i, pl.ds(row, FRAME), :], back_shift, 1)
                for i in range(3)
            ]
            return [jnp.where(keep, rolled[i], rolled[i + 1]) for i in range(2)]

        patch_re = cut(0)
        patch_im = cut(1)
        ex_re, ex_im = [], []
        for h in range(2):
            lanes = slice(128 * h, 128 * h + 128)
            pr = probe_ref[0, :, lanes]
            pi = probe_ref[1, :, lanes]
            ex_re.append(pr * patch_re[h] - pi * patch_im[h])
            ex_im.append(pr * patch_im[h] + pi * patch_re[h])
        xs[0, rows_of[m], 0:128] = (ex_re[0] + ex_re[1]).astype(BF16)
        xs[0, rows_of[m], 128:256] = (ex_im[0] + ex_im[1]).astype(BF16)
        xs[1, rows_of[m], 0:128] = (ex_re[0] - ex_re[1]).astype(BF16)
        xs[1, rows_of[m], 128:256] = (ex_im[0] - ex_im[1]).astype(BF16)
    halves = [dot(xs[q], table_ref[q]) for q in range(2)]
    for m in members:
        for q in range(2):
            half = halves[q][rows_of[m]]
            top, bottom = half[:HALF], half[HALF:]
            lanes = slice(128 * q, 128 * q + 128)
            for p, fold in ((0, top + bottom), (1, top - bottom)):
                folded = fold.astype(BF16)
                gs[m, p, 0:HALF, lanes] = folded[:, :128]
                gs[m, p, HALF:, lanes] = folded[:, 128:]
    for m in members:
        for p in range(2):
            far = dot(table_ref[2 + p], gs[m, p])
            rows = slice(FRAME * m + HALF * p, FRAME * m + HALF * p + HALF)
            for q in range(2):
                lanes = slice(128 * q, 128 * q + 128)
                far_re, far_im = far[:HALF, lanes], far[HALF:, lanes]
                a = amp_ref[m, FRAME * q + HALF * p : FRAME * q + HALF * p + HALF, :].astype(F32)
                factor = a * lax.rsqrt(far_re * far_re + far_im * far_im + 1.0) - 1.0
                ds[q, rows, 0:128] = (far_re * factor).astype(BF16)
                ds[q, rows, 128:256] = (far_im * factor).astype(BF16)
    evens = dot(ds[0], table_ref[4])
    odds = dot(ds[1], table_ref[5])
    for m in members:
        even, odd = evens[rows_of[m]], odds[rows_of[m]]
        for h, mid in ((0, (even + odd).astype(BF16)), (1, (even - odd).astype(BF16))):
            lanes = slice(128 * h, 128 * h + 128)
            for p in range(2):
                rows = slice(HALF * p, HALF * p + HALF)
                ms[m, p, 0:HALF, lanes] = mid[rows, :128]
                ms[m, p, HALF:, lanes] = mid[rows, 128:]
    for m in members:
        row, col, live = places[m]
        shift = col % 128
        panel = jnp.where(live > 0, col // 128, PANELS)
        even = dot(table_ref[6], ms[m, 0])
        odd = dot(table_ref[7], ms[m, 1])
        keep = lane[:HALF] < shift
        for v in range(2):
            back = even + odd if v == 0 else even - odd
            back_re, back_im = back[:HALF], back[HALF:]
            rows = slice(HALF * v, HALF * v + HALF)
            pr = probe_ref[0, rows]
            pi = probe_ref[1, rows]
            where = pl.ds(row + HALF * v, HALF)
            for part, term in ((0, pr * back_re + pi * back_im), (1, pr * back_im - pi * back_re)):
                left = pltpu.roll(term[:, :128], shift, 1)
                right = pltpu.roll(term[:, 128:], shift, 1)
                acc_ref[part, panel, where, :] += jnp.where(keep, 0.0, left)
                acc_ref[part, panel + 1, where, :] += jnp.where(keep, left, right)
                acc_ref[part, panel + 2, where, :] += jnp.where(keep, right, 0.0)


def run_group(rank, meta_ref, amp_ref, probe_ref, table_ref, ext_ref, acc_ref, *scratch):
    step = pl.program_id(0)
    places = [[meta_ref[3 * rank + k, step * GROUP + m] for k in range(3)] for m in range(GROUP)]
    live = places[0][2]
    for place in places[1:]:
        live = live + place[2]

    @pl.when(live > 0)
    def _():
        process(places, amp_ref, probe_ref, table_ref, ext_ref, acc_ref, *scratch)


def first_kernel(meta_ref, amp_ref, probe_ref, table_ref, ext_ref, out_ref, acc_ref, *scratch):
    step = pl.program_id(0)

    @pl.when(step == 0)
    def _():
        acc_ref[:, 0:PANELS] = jnp.zeros_like(out_ref)

    run_group(0, meta_ref, amp_ref, probe_ref, table_ref, ext_ref, acc_ref, *scratch)

    @pl.when(step == pl.num_programs(0) - 1)
    def _():
        out_ref[...] = acc_ref[:, 0:PANELS]


def last_kernel(
    meta_ref, amp_ref, probe_ref, table_ref, ext_ref, start_ref,
    west_ref, east_ref, mid_ref, acc_ref, *scratch,
):
    step = pl.program_id(0)

    @pl.when(step == 0)
    def _():
        acc_ref[:, 0:PANELS] = start_ref[...]

    run_group(1, meta_ref, amp_ref, probe_ref, table_ref, ext_ref, acc_ref, *scratch)

    @pl.when(step == pl.num_programs(0) - 1)
    def _():
        for part in range(2):
            west_ref[part] = (0.5 * acc_ref[part, 0]).astype(BF16)
            east_ref[part] = (0.5 * acc_ref[part, PANELS - 1]).astype(BF16)
            for j in range(TILE // 128):
                lanes = slice(128 * j, 128 * j + 128)
                inner = slice(HALF, HALF + TILE)
                mid_ref[part, 0:HALF, lanes] = 0.5 * acc_ref[part, j + 1, 0:HALF, :]
                mid_ref[part, inner, lanes] = (
                    ext_ref[part, j + 1, inner, :] + 0.5 * acc_ref[part, j + 1, inner, :]
                )
                mid_ref[part, HALF + TILE :, lanes] = 0.5 * acc_ref[part, j + 1, HALF + TILE :, :]


def whole(shape):
    return pl.BlockSpec(shape, lambda s, m: (0,) * len(shape))


def run_slots(meta, amps, probe, tabs, ext, acc=None):
    slots = amps.shape[0]
    wide = (2, PANELS, EXTENT, 128)
    in_specs = [
        pl.BlockSpec((GROUP,) + amps.shape[1:], lambda s, m: (s, 0, 0)),
        whole((2, FRAME, FRAME)),
        whole((8, FRAME, FRAME)),
        whole(wide),
    ]
    operands = [meta, amps, probe, tabs, ext]
    rows, cols = (2, GROUP * FRAME, FRAME), (GROUP, 2, FRAME, FRAME)
    scratch = [pltpu.VMEM((2, PANELS + 3, EXTENT, 128), F32)]
    scratch += [pltpu.VMEM(shape, BF16) for shape in (rows, cols, rows, cols)]
    if acc is None:
        kernel = first_kernel
        out_shape = jax.ShapeDtypeStruct(wide, F32)
        out_specs = whole(wide)
    else:
        kernel = last_kernel
        in_specs.append(whole(wide))
        operands.append(acc)
        shapes = [(2, EXTENT, 128), (2, EXTENT, 128), (2, EXTENT, TILE)]
        out_shape = [jax.ShapeDtypeStruct(s, d) for s, d in zip(shapes, (BF16, BF16, F32))]
        out_specs = [whole(s) for s in shapes]
    return pl.pallas_call(
        kernel,
        grid_spec=pltpu.PrefetchScalarGridSpec(
            num_scalar_prefetch=1,
            grid=(slots // GROUP,),
            in_specs=in_specs,
            out_specs=out_specs,
            scratch_shapes=scratch,
        ),
        out_shape=out_shape,
        compiler_params=pltpu.CompilerParams(vmem_limit_bytes=56 << 20),
        cost_estimate=pl.CostEstimate(
            flops=slots * 16 * FRAME**3, bytes_accessed=16 << 20, transcendentals=0
        ),
        name="slots",
    )(*operands)


def finish_kernel(base_ref, strip_ref, out_ref):
    out_ref[...] = base_ref[...] + strip_ref[0].astype(F32)


def shifted(value, axis, by):
    size = lax.axis_size(axis)
    pairs = [(i, i + by) for i in range(size) if 0 <= i + by < size]
    return lax.ppermute(value, axis, pairs)


def body(obj, probe, intensity, dest, offsets):
    groups = lax.axis_size("gx")
    sends = prep(dest[:, 0], offsets.reshape(-1), intensity, groups)
    north = shifted(obj[:, TILE - HALF :, :].astype(BF16), "gy", 1)
    south = shifted(obj[:, :HALF, :].astype(BF16), "gy", -1)
    amps = [lax.all_to_all(s, "gx", split_axis=0, concat_axis=0, tiled=True) for s in sends]

    def column(lo, hi):
        own = obj[:, :, lo:hi].astype(BF16)
        return jnp.concatenate([north[:, :, lo:hi], own, south[:, :, lo:hi]], axis=1)

    west = shifted(column(TILE - HALF, TILE), "gx", 1)
    east = shifted(column(0, HALF), "gx", -1)
    ext = assemble(obj, north, south, west, east)
    tabs = jnp.asarray(table_blocks())
    notes = amps[0][:, 2 * FRAME, :10].astype(jnp.int32).T
    meta = jnp.stack(
        [
            notes[5 * r] * 16 + notes[5 * r + 1] if k == 0 else
            notes[5 * r + 2] * 16 + notes[5 * r + 3] if k == 1 else notes[5 * r + 4]
            for r in range(CAP) for k in range(3)
        ]
    )
    acc = run_slots(meta, amps[0], probe, tabs, ext)
    west, east, mid = run_slots(meta, amps[1], probe, tabs, ext, acc)
    from_west = shifted(east, "gx", 1).astype(F32)
    from_east = shifted(west, "gx", -1).astype(F32)

    def summed(lo, hi):
        rows = mid[:, lo:hi]
        left = rows[:, :, :HALF] + from_west[:, lo:hi]
        right = rows[:, :, TILE - HALF :] + from_east[:, lo:hi]
        return jnp.concatenate([left, rows[:, :, HALF : TILE - HALF], right], axis=2)

    to_north = summed(0, HALF).astype(BF16)
    to_south = summed(HALF + TILE, EXTENT).astype(BF16)
    from_north = shifted(to_south, "gy", 1)
    from_south = shifted(to_north, "gy", -1)
    inner = summed(HALF, HALF + TILE)
    strips = jnp.stack([from_north, from_south])
    return pl.pallas_call(
        finish_kernel,
        grid=(2,),
        in_specs=[
            pl.BlockSpec((2, HALF, TILE), lambda i: (0, 3 * i, 0)),
            pl.BlockSpec((1, 2, HALF, TILE), lambda i: (i, 0, 0, 0)),
        ],
        out_specs=pl.BlockSpec((2, HALF, TILE), lambda i: (0, 3 * i, 0)),
        out_shape=jax.ShapeDtypeStruct((2, TILE, TILE), F32),
        input_output_aliases={0: 0},
        name="finish",
    )(inner, strips)


def solution(mesh):
    placed = (
        P(None, "gy", "gx"),
        P(),
        P(("gx", "gy"), None, None),
        P(("gx", "gy"), None),
        P(("gx", "gy"), None),
    )
    return jax.shard_map(
        body, mesh=mesh, in_specs=placed, out_specs=P(None, "gy", "gx"), check_vma=False
    )
```

time: 209 us -> 161 us (0.77)
  the two profiles are of different devices: /device:TPU:120 before, /device:TPU:105 now
where the time goes in v1:
time: 161 us
  waiting for transfers between devices  59.6 us (37%)
  Pallas kernels  48.8 us (30%)
  starting transfers between devices  39.4 us (24%)
  local copies, waits for them, and re-layouts  7.45 us (5%)
  other arithmetic  5.26 us (3%)
    pallas_call x2, Pallas kernels, run_slots(): pl.pallas_call(kernel, grid_spec=pltpu.PrefetchScalarGridSpec(num_scalar_...  38.6 us
    ppermute x8, waiting for transfers between devices, shifted(): return lax.ppermute(value, axis, pairs)  37.7 us
    ppermute x8, starting transfers between devices, shifted(): return lax.ppermute(value, axis, pairs)  24.1 us
    all_to_all x2, waiting for transfers between devices, body(): lax.all_to_all(s, 'gx', split_axis=0, concat_axis=0, tiled=True)  21.9 us
    all_to_all x2, starting transfers between devices, body(): lax.all_to_all(s, 'gx', split_axis=0, concat_axis=0, tiled=True)  15.3 us
    pallas_call x1, Pallas kernels, prep(): pl.pallas_call(prep_kernel, grid_spec=pltpu.PrefetchScalarGridSpec(num_sc...  7.65 us
  transfers between devices with their start and end apart: 10, of which 7 were waited for; matrix products, arithmetic and copies ran while one was open for 5% of the time, Pallas kernels for 12%

profile of v1, /device:TPU:105, one launch (start us, length us, event | category | flops | bytes accessed | tf_op | source)
XLA Modules:
  0.0 160.7 jit_solution(14875996900576942798)
XLA Ops:
  0.0 0.8 copy.15
  0.8 0.6 reshape.5.offs_ref
  1.3 7.6 %prep.1 = (bf16[16,528,128]{2,1,0:T(8,128)(2,1)}, bf16[16,512,128]{2,1,0:T(8,128)(2,1)}) custom-call(s32[16]{0:T(128)} %bitcast.10, s32[32]{0:T(128)} %reshape.5.offs_ref, f32[16,256,256]{2,1,0:T(8,128)} %right_ref.1, f32[16,256,256]{2,1,0:T(8,128)} %right_ref.1, bf16[256,256]{1,0:T(8,128)(2,1)} %constant.6.clone.perm_ref), custom_call_target="tpu_custom_call" | custom-call | flops 536870912 | bytes 6291456 | tf_op jit(solution)/shard_map/prep/pallas_call | solution.py:136
  9.0 0.0 copy-start
  9.0 7.9 %all-to-all-start = ((bf16[16,528,128]{2,1,0:T(8,128)(2,1)}), bf16[16,528,128]{2,1,0:T(8,128)(2,1)}, u32[]{:S(2)}, u32[]{:S(2)}) async-start(bf16[16,528,128]{2,1,0:T(8,128)(2,1)} %get-tuple-element.10), calls=%async_computation | async-start | bytes 4325376 | tf_op jit(solution)/shard_map/all_to_all | solution.py:385
  16.9 0.0 copy-done
  16.9 0.1 convert.26
  17.0 0.0 copy-start.3
  17.1 2.0 %collective-permute-start.1 = (bf16[2,128,512]{2,1,0:T(8,128)(2,1)S(1)}, bf16[2,128,512]{2,1,0:T(8,128)(2,1)S(1)}, u32[]{:S(2)}, u32[]{:S(2)}) collective-permute-start(bf16[2,128,512]{2,1,0:T(8,128)(2,1)S(1)} %get-tuple-element.27), channel_id=1, source_target_pairs={{1,0},{2,1},{3,2},{4,3},{5,4},{6,5},{7,6},{9,8},{10,9},{11,10},{12... | collective-permute-start | bytes 786440 | tf_op jit(solution)/shard_map/ppermute | solution.py:377
  19.1 0.0 copy-done.3
  19.1 3.2 %collective-permute-start = (bf16[2,128,512]{2,1,0:T(8,128)(2,1)S(1)}, bf16[2,128,512]{2,1,0:T(8,128)(2,1)S(1)}, u32[]{:S(2)}, u32[]{:S(2)}) collective-permute-start(bf16[2,128,512]{2,1,0:T(8,128)(2,1)S(1)} %get-tuple-element.28), channel_id=1, source_target_pairs={{0,1},{1,2},{2,3},{3,4},{4,5},{5,6},{6,7},{8,9},{9,10},{10,11},{11... | collective-permute-start | bytes 786440 | tf_op jit(solution)/shard_map/ppermute | solution.py:377
  22.4 21.9 %all-to-all-done.amp_ref = bf16[16,528,128]{2,1,0:T(8,128)(2,1)} async-done(((bf16[16,528,128]{2,1,0:T(8,128)(2,1)}), bf16[16,528,128]{2,1,0:T(8,128)(2,1)}, u32[]{:S(2)}, u32[]{:S(2)}) %all-to-all-start) | async-done | bytes 2162720 | tf_op jit(solution)/shard_map/all_to_all | solution.py:385
  44.3 7.4 %all-to-all-start.1 = ((bf16[16,512,128]{2,1,0:T(8,128)(2,1)}), bf16[16,512,128]{2,1,0:T(8,128)(2,1)}, u32[]{:S(2)}, u32[]{:S(2)}) async-start(bf16[16,512,128]{2,1,0:T(8,128)(2,1)} %get-tuple-element.11), calls=%async_computation.1 | async-start | bytes 4194304 | tf_op jit(solution)/shard_map/all_to_all | solution.py:385
  51.7 1.1 fusion.5
  52.8 0.0 collective-permute-done.1.south_ref
  52.8 0.0 collective-permute-done.north_ref
  52.9 6.2 %collective-permute-start.2 = (bf16[2,768,128]{2,1,0:T(8,128)(2,1)S(1)}, bf16[2,768,128]{2,1,0:T(8,128)(2,1)S(1)}, u32[]{:S(2)}, u32[]{:S(2)}) collective-permute-start(bf16[2,768,128]{2,1,0:T(8,128)(2,1)S(1)} %pad_maximum_fusion.2), channel_id=1, source_target_pairs={{0,8},{8,16},{16,24},{24,32},{32,40},{40,48},{48,56},{56,64},{64,7... | collective-permute-start | bytes 1179656 | tf_op jit(solution)/shard_map/ppermute | solution.py:377
  59.1 1.9 %collective-permute-start.3 = (bf16[2,768,128]{2,1,0:T(8,128)(2,1)S(1)}, bf16[2,768,128]{2,1,0:T(8,128)(2,1)S(1)}, u32[]{:S(2)}, u32[]{:S(2)}) collective-permute-start(bf16[2,768,128]{2,1,0:T(8,128)(2,1)S(1)} %pad_maximum_fusion.3), channel_id=1, source_target_pairs={{8,0},{16,8},{24,16},{32,24},{40,32},{48,40},{56,48},{64,56},{72,6... | collective-permute-start | bytes 1179656 | tf_op jit(solution)/shard_map/ppermute | solution.py:377
  61.0 21.9 %collective-permute-done.2.west_ref = bf16[2,768,128]{2,1,0:T(8,128)(2,1)S(1)} collective-permute-done((bf16[2,768,128]{2,1,0:T(8,128)(2,1)S(1)}, bf16[2,768,128]{2,1,0:T(8,128)(2,1)S(1)}, u32[]{:S(2)}, u32[]{:S(2)}) %collective-permute-start.2) | collective-permute-done | bytes 393248 | tf_op jit(solution)/shard_map/ppermute | solution.py:377
  82.9 3.8 %collective-permute-done.3.east_ref = bf16[2,768,128]{2,1,0:T(8,128)(2,1)S(1)} collective-permute-done((bf16[2,768,128]{2,1,0:T(8,128)(2,1)S(1)}, bf16[2,768,128]{2,1,0:T(8,128)(2,1)S(1)}, u32[]{:S(2)}, u32[]{:S(2)}) %collective-permute-start.3) | collective-permute-done | bytes 393248 | tf_op jit(solution)/shard_map/ppermute | solution.py:377
  86.7 0.3 assemble.1.ext_ref
  87.0 0.0 copy-start.1
  87.0 2.1 %copy-done.1 = f32[2,6,768,128]{3,2,1,0:T(8,128)} copy-done((f32[2,6,768,128]{3,2,1,0:T(8,128)}, f32[2,6,768,128]{3,2,1,0:T(8,128)S(1)}, u32[]{:S(2)}) %copy-start.1) | copy-done | bytes 4718616
  89.2 0.8 slice.154
  89.9 0.1 copy.17
  90.1 0.6 stack.16.meta_ref
  90.7 18.6 %slots.2.start_ref = f32[2,6,768,128]{3,2,1,0:T(8,128)} custom-call(s32[6,16]{1,0:T(8,128)} %stack.16.meta_ref, bf16[16,528,128]{2,1,0:T(8,128)(2,1)} %all-to-all-done.amp_ref, f32[2,256,256]{2,1,0:T(8,128)} %probe_ref.3, bf16[8,256,256]{2,1,0:T(8,128)(2,1)} %constant.7.clone.table_ref, f32[2,6,768,128]{3,2,1,0:T(8,128)} %copy-done.1), custom_call_target="tpu_custom_call" | custom-call | flops 4294967296 | bytes 16777216 | tf_op jit(solution)/shard_map/slots/pallas_call | solution.py:352
  109.2 0.0 all-to-all-done.1.amp_ref
  109.2 20.0 %slots.3 = (bf16[2,768,128]{2,1,0:T(8,128)(2,1)}, bf16[2,768,128]{2,1,0:T(8,128)(2,1)}, f32[2,768,512]{2,1,0:T(8,128)}) custom-call(s32[6,16]{1,0:T(8,128)} %stack.16.meta_ref, bf16[16,512,128]{2,1,0:T(8,128)(2,1)} %all-to-all-done.1.amp_ref, f32[2,256,256]{2,1,0:T(8,128)} %probe_ref.3, bf16[8,256,256]{2,1,0:T(8,128)(2,1)} %constant.7.clone.table_ref, ...), custom_call_target="tpu_custom_call" | custom-call | flops 4294967296 | bytes 16777216 | tf_op jit(solution)/shard_map/slots/pallas_call | solution.py:352
  129.3 1.9 %collective-permute-start.4 = (bf16[2,768,128]{2,1,0:T(8,128)(2,1)}, bf16[2,768,128]{2,1,0:T(8,128)(2,1)S(1)}, u32[]{:S(2)}, u32[]{:S(2)}) collective-permute-start(bf16[2,768,128]{2,1,0:T(8,128)(2,1)} %get-tuple-element.13), channel_id=1, source_target_pairs={{0,8},{8,16},{16,24},{24,32},{32,40},{40,48},{48,56},{56,64},{64,7... | collective-permute-start | bytes 1179656 | tf_op jit(solution)/shard_map/ppermute | solution.py:377
  131.2 2.4 %collective-permute-start.5 = (bf16[2,768,128]{2,1,0:T(8,128)(2,1)}, bf16[2,768,128]{2,1,0:T(8,128)(2,1)S(1)}, u32[]{:S(2)}, u32[]{:S(2)}) collective-permute-start(bf16[2,768,128]{2,1,0:T(8,128)(2,1)} %get-tuple-element.14), channel_id=1, source_target_pairs={{8,0},{16,8},{24,16},{32,24},{40,32},{48,40},{56,48},{64,56},{72,6... | collective-permute-start | bytes 1179656 | tf_op jit(solution)/shard_map/ppermute | solution.py:377
  133.6 1.3 slice.141
  134.9 0.0 copy-start.2
  135.0 2.2 %convert.28 = bf16[2,768,512]{2,1,0:T(8,128)(2,1)S(1)} convert(f32[2,768,512]{2,1,0:T(8,128)} %get-tuple-element.12) | non-fusion elementwise | flops 786432 | bytes 4718592 | tf_op jit(solution)/shard_map/convert.9
  137.2 0.5 collective-permute-done.4
  137.8 0.1 convert_element_type.8
  137.8 5.8 %collective-permute-done.5 = bf16[2,768,128]{2,1,0:T(8,128)(2,1)S(1)} collective-permute-done((bf16[2,768,128]{2,1,0:T(8,128)(2,1)}, bf16[2,768,128]{2,1,0:T(8,128)(2,1)S(1)}, u32[]{:S(2)}, u32[]{:S(2)}) %collective-permute-start.5) | collective-permute-done | bytes 393248 | tf_op jit(solution)/shard_map/ppermute | solution.py:377
  143.6 0.1 convert_element_type.18
  143.6 0.0 copy-done.2
  143.7 0.1 fusion.3
  143.8 4.5 %collective-permute-start.7 = (bf16[2,128,512]{2,1,0:T(8,128)(2,1)S(1)}, bf16[2,128,512]{2,1,0:T(8,128)(2,1)S(1)}, u32[]{:S(2)}, u32[]{:S(2)}) collective-permute-start(bf16[2,128,512]{2,1,0:T(8,128)(2,1)S(1)} %pad_maximum_fusion.5), channel_id=1, source_target_pairs={{1,0},{2,1},{3,2},{4,3},{5,4},{6,5},{7,6},{9,8},{10,9},{11,10},{12... | collective-permute-start | bytes 786440 | tf_op jit(solution)/shard_map/ppermute | solution.py:377
  148.3 1.9 %collective-permute-start.6 = (bf16[2,128,512]{2,1,0:T(8,128)(2,1)S(1)}, bf16[2,128,512]{2,1,0:T(8,128)(2,1)S(1)}, u32[]{:S(2)}, u32[]{:S(2)}) collective-permute-start(bf16[2,128,512]{2,1,0:T(8,128)(2,1)S(1)} %pad_maximum_fusion.4), channel_id=1, source_target_pairs={{0,1},{1,2},{2,3},{3,4},{4,5},{5,6},{6,7},{8,9},{9,10},{10,11},{11... | collective-permute-start | bytes 786440 | tf_op jit(solution)/shard_map/ppermute | solution.py:377
  150.3 0.1 slice_add_fusion.1
  150.4 1.5 pad_maximum_fusion.base_ref
  152.0 1.3 collective-permute-done.7
  153.3 4.4 %collective-permute-done.6 = bf16[2,128,512]{2,1,0:T(8,128)(2,1)S(1)} collective-permute-done((bf16[2,128,512]{2,1,0:T(8,128)(2,1)S(1)}, bf16[2,128,512]{2,1,0:T(8,128)(2,1)S(1)}, u32[]{:S(2)}, u32[]{:S(2)}) %collective-permute-start.6) | collective-permute-done | bytes 262176 | tf_op jit(solution)/shard_map/ppermute | solution.py:377
  157.7 0.9 pad_maximum_fusion.1.strip_ref
  158.5 2.2 %finish.1 = f32[2,512,512]{2,1,0:T(8,128)} custom-call(f32[2,512,512]{2,1,0:T(8,128)} %pad_maximum_fusion.base_ref, bf16[2,2,128,512]{3,2,1,0:T(8,128)(2,1)} %pad_maximum_fusion.1.strip_ref), custom_call_target="tpu_custom_call", output_to_operand_aliasing={{}: (0, {})} | custom-call | tf_op jit(solution)/shard_map/finish/pallas_call | solution.py:420
  (10 shorter events, 0.3 us)
Async XLA Ops:
  9.0 7.9 %copy-start = (f32[2,512,512]{2,1,0:T(8,128)S(1)}, f32[2,512,512]{2,1,0:T(8,128)}, u32[]{:S(2)}) copy-start(f32[2,512,512]{2,1,0:T(8,128)} %obj_ref.1) | copy-start | bytes 6291460
  9.0 35.2 %all-to-all-start = ((bf16[16,528,128]{2,1,0:T(8,128)(2,1)}), bf16[16,528,128]{2,1,0:T(8,128)(2,1)}, u32[]{:S(2)}, u32[]{:S(2)}) async-start(bf16[16,528,128]{2,1,0:T(8,128)(2,1)} %get-tuple-element.10), calls=%async_computation | async-start | bytes 4325376 | tf_op jit(solution)/shard_map/all_to_all | solution.py:385
  17.0 2.1 %copy-start.3 = (bf16[2,512,512]{2,1,0:T(8,128)(2,1)}, bf16[2,512,512]{2,1,0:T(8,128)(2,1)S(1)}, u32[]{:S(2)}) copy-start(bf16[2,512,512]{2,1,0:T(8,128)(2,1)S(1)} %convert.26) | copy-start | bytes 3145732
  17.1 35.7 %collective-permute-start.1 = (bf16[2,128,512]{2,1,0:T(8,128)(2,1)S(1)}, bf16[2,128,512]{2,1,0:T(8,128)(2,1)S(1)}, u32[]{:S(2)}, u32[]{:S(2)}) collective-permute-start(bf16[2,128,512]{2,1,0:T(8,128)(2,1)S(1)} %get-tuple-element.27), channel_id=1, source_target_pairs={{1,0},{2,1},{3,2},{4,3},{5,4},{6,5},{7,6},{9,8},{10,9},{11,10},{12... | collective-permute-start | bytes 786440 | tf_op jit(solution)/shard_map/ppermute | solution.py:377
  19.1 33.7 %collective-permute-start = (bf16[2,128,512]{2,1,0:T(8,128)(2,1)S(1)}, bf16[2,128,512]{2,1,0:T(8,128)(2,1)S(1)}, u32[]{:S(2)}, u32[]{:S(2)}) collective-permute-start(bf16[2,128,512]{2,1,0:T(8,128)(2,1)S(1)} %get-tuple-element.28), channel_id=1, source_target_pairs={{0,1},{1,2},{2,3},{3,4},{4,5},{5,6},{6,7},{8,9},{9,10},{10,11},{11... | collective-permute-start | bytes 786440 | tf_op jit(solution)/shard_map/ppermute | solution.py:377
  44.3 65.0 %all-to-all-start.1 = ((bf16[16,512,128]{2,1,0:T(8,128)(2,1)}), bf16[16,512,128]{2,1,0:T(8,128)(2,1)}, u32[]{:S(2)}, u32[]{:S(2)}) async-start(bf16[16,512,128]{2,1,0:T(8,128)(2,1)} %get-tuple-element.11), calls=%async_computation.1 | async-start | bytes 4194304 | tf_op jit(solution)/shard_map/all_to_all | solution.py:385
  52.9 30.0 %collective-permute-start.2 = (bf16[2,768,128]{2,1,0:T(8,128)(2,1)S(1)}, bf16[2,768,128]{2,1,0:T(8,128)(2,1)S(1)}, u32[]{:S(2)}, u32[]{:S(2)}) collective-permute-start(bf16[2,768,128]{2,1,0:T(8,128)(2,1)S(1)} %pad_maximum_fusion.2), channel_id=1, source_target_pairs={{0,8},{8,16},{16,24},{24,32},{32,40},{40,48},{48,56},{56,64},{64,7... | collective-permute-start | bytes 1179656 | tf_op jit(solution)/shard_map/ppermute | solution.py:377
  59.1 27.6 %collective-permute-start.3 = (bf16[2,768,128]{2,1,0:T(8,128)(2,1)S(1)}, bf16[2,768,128]{2,1,0:T(8,128)(2,1)S(1)}, u32[]{:S(2)}, u32[]{:S(2)}) collective-permute-start(bf16[2,768,128]{2,1,0:T(8,128)(2,1)S(1)} %pad_maximum_fusion.3), channel_id=1, source_target_pairs={{8,0},{16,8},{24,16},{32,24},{40,32},{48,40},{56,48},{64,56},{72,6... | collective-permute-start | bytes 1179656 | tf_op jit(solution)/shard_map/ppermute | solution.py:377
  87.0 2.1 %copy-start.1 = (f32[2,6,768,128]{3,2,1,0:T(8,128)}, f32[2,6,768,128]{3,2,1,0:T(8,128)S(1)}, u32[]{:S(2)}) copy-start(f32[2,6,768,128]{3,2,1,0:T(8,128)S(1)} %assemble.1.ext_ref) | copy-start | bytes 14155780
  129.3 8.5 %collective-permute-start.4 = (bf16[2,768,128]{2,1,0:T(8,128)(2,1)}, bf16[2,768,128]{2,1,0:T(8,128)(2,1)S(1)}, u32[]{:S(2)}, u32[]{:S(2)}) collective-permute-start(bf16[2,768,128]{2,1,0:T(8,128)(2,1)} %get-tuple-element.13), channel_id=1, source_target_pairs={{0,8},{8,16},{16,24},{24,32},{32,40},{40,48},{48,56},{56,64},{64,7... | collective-permute-start | bytes 1179656 | tf_op jit(solution)/shard_map/ppermute | solution.py:377
  131.2 12.4 %collective-permute-start.5 = (bf16[2,768,128]{2,1,0:T(8,128)(2,1)}, bf16[2,768,128]{2,1,0:T(8,128)(2,1)S(1)}, u32[]{:S(2)}, u32[]{:S(2)}) collective-permute-start(bf16[2,768,128]{2,1,0:T(8,128)(2,1)} %get-tuple-element.14), channel_id=1, source_target_pairs={{8,0},{16,8},{24,16},{32,24},{40,32},{48,40},{56,48},{64,56},{72,6... | collective-permute-start | bytes 1179656 | tf_op jit(solution)/shard_map/ppermute | solution.py:377
  134.9 8.7 %copy-start.2 = (f32[2,768,512]{2,1,0:T(8,128)S(1)}, f32[2,768,512]{2,1,0:T(8,128)}, u32[]{:S(2)}) copy-start(f32[2,768,512]{2,1,0:T(8,128)} %get-tuple-element.12) | copy-start | bytes 9437188
  143.8 9.5 %collective-permute-start.7 = (bf16[2,128,512]{2,1,0:T(8,128)(2,1)S(1)}, bf16[2,128,512]{2,1,0:T(8,128)(2,1)S(1)}, u32[]{:S(2)}, u32[]{:S(2)}) collective-permute-start(bf16[2,128,512]{2,1,0:T(8,128)(2,1)S(1)} %pad_maximum_fusion.5), channel_id=1, source_target_pairs={{1,0},{2,1},{3,2},{4,3},{5,4},{6,5},{7,6},{9,8},{10,9},{11,10},{12... | collective-permute-start | bytes 786440 | tf_op jit(solution)/shard_map/ppermute | solution.py:377
  148.3 9.3 %collective-permute-start.6 = (bf16[2,128,512]{2,1,0:T(8,128)(2,1)S(1)}, bf16[2,128,512]{2,1,0:T(8,128)(2,1)S(1)}, u32[]{:S(2)}, u32[]{:S(2)}) collective-permute-start(bf16[2,128,512]{2,1,0:T(8,128)(2,1)S(1)} %pad_maximum_fusion.4), channel_id=1, source_target_pairs={{0,1},{1,2},{2,3},{3,4},{4,5},{5,6},{6,7},{8,9},{9,10},{10,11},{11... | collective-permute-start | bytes 786440 | tf_op jit(solution)/shard_map/ppermute | solution.py:377

commit v2 on v1

v2 whole, which is shorter than its diff:
```python
import functools
import math

import jax
import jax.numpy as jnp
import numpy as np
from jax import lax
from jax.experimental import pallas as pl
from jax.experimental.pallas import tpu as pltpu
from jax.sharding import PartitionSpec as P

CAP = 2
FRAME = 256
HALF = 128
TILE = 512
EXTENT = TILE + 2 * HALF
PANELS = EXTENT // 128
NOTE_ROWS = 16
GROUP = 4
BF16 = jnp.bfloat16
F32 = jnp.float32


def table_blocks():
    index = np.arange(FRAME)[:, None] * np.arange(FRAME)[None, :] % FRAME
    angle = index.astype(np.float32) * np.float32(2.0 * math.pi / FRAME)
    scale = np.float32(1.0 / math.sqrt(FRAME))
    re = (np.cos(angle) * scale).astype(BF16)
    im = (-np.sin(angle) * scale).astype(BF16)
    blocks = []
    for parity in (0, 1):
        c = re[:HALF, parity::2]
        s = im[:HALF, parity::2]
        fwd_right = np.block([[c, s], [-s, c]])
        fwd_left = fwd_right.T
        inv_right = np.block([[c.T, -s.T], [s.T, c.T]])
        inv_left = inv_right.T
        blocks.append([fwd_right, fwd_left, inv_right, inv_left])
    return np.stack([blocks[p][i] for i in range(4) for p in (0, 1)]).astype(BF16)


def deinterleave():
    perm = np.zeros((FRAME, FRAME), np.float32)
    for j in range(HALF):
        perm[2 * j, j] = 1.0
        perm[2 * j + 1, HALF + j] = 1.0
    return perm.astype(BF16)


def dot(a, b):
    return jnp.dot(a, b, preferred_element_type=F32)


def prep_kernel(
    where_ref, inten_ref, perm_ref, first_ref, second_ref, stage, split, notes, ranks, sems
):
    step = pl.program_id(0)
    count = pl.num_programs(0)
    per = inten_ref.shape[0]
    groups = first_ref.shape[0]
    slot = step % 2

    def notes_copy():
        return pltpu.make_async_copy(
            notes, first_ref.at[:, pl.ds(2 * FRAME, NOTE_ROWS), :], sems.at[2 * per]
        )

    @pl.when(step == 0)
    def _():
        lane = lax.broadcasted_iota(jnp.int32, (groups, 128), 1)
        owner = lax.broadcasted_iota(jnp.int32, (groups, 128), 0)
        note = jnp.zeros((groups, 128), jnp.int32)
        for g in range(groups):
            ranks[per * count + g] = 0
        for f in range(per * count):
            mine = where_ref[f]
            rank = ranks[per * count + mine]
            ranks[f] = rank
            ranks[per * count + mine] = rank + 1
            row, col = where_ref[per * count + f], where_ref[2 * per * count + f]
            at = lane - 5 * rank
            value = jnp.where(at == 0, row // 16, jnp.where(at == 1, row % 16, 0))
            value += jnp.where(at == 2, col // 16, jnp.where(at == 3, col % 16, 0))
            value += jnp.where(at == 4, 1, 0)
            note = jnp.where(owner == mine, note + value, note)
        notes[...] = jnp.broadcast_to(note.astype(F32)[:, None, :], notes.shape).astype(BF16)
        notes_copy().start()

    for i in range(per):

        @pl.when(step >= 2)
        def _():
            pltpu.make_async_copy(
                stage.at[slot, i], second_ref.at[0], sems.at[slot * per + i]
            ).wait()

    for i in range(per):
        for h in range(2):
            split[i, h] = jnp.sqrt(inten_ref[i, :, 128 * h : 128 * h + 128])
        rows = [
            jnp.concatenate([split[i, h, pl.ds(p, HALF, 2), :] for h in range(2)], axis=1)
            for p in range(2)
        ]
        amp = jnp.concatenate(rows, axis=0).astype(BF16)
        cols = dot(amp, perm_ref[...]).astype(BF16)
        stage[slot, i, 0:FRAME, :] = cols[:, :128]
        stage[slot, i, FRAME : 2 * FRAME, :] = cols[:, 128:]
    for i in range(per):
        f = step * per + i
        mine = where_ref[f]
        rank = ranks[f]

        @pl.when(rank == 0)
        def _():
            pltpu.make_async_copy(
                stage.at[slot, i],
                first_ref.at[mine, pl.ds(0, 2 * FRAME), :],
                sems.at[slot * per + i],
            ).start()

        @pl.when(rank != 0)
        def _():
            pltpu.make_async_copy(
                stage.at[slot, i], second_ref.at[mine], sems.at[slot * per + i]
            ).start()

    @pl.when(step == count - 1)
    def _():
        notes_copy().wait()
        for s in range(2):
            for i in range(per):
                pltpu.make_async_copy(
                    stage.at[s, i], second_ref.at[0], sems.at[s * per + i]
                ).wait()


def prep(where, intensity, groups):
    frames = intensity.shape[0]
    per = 4
    return pl.pallas_call(
        prep_kernel,
        grid_spec=pltpu.PrefetchScalarGridSpec(
            num_scalar_prefetch=1,
            grid=(frames // per,),
            in_specs=[
                pl.BlockSpec((per, FRAME, FRAME), lambda s, w: (s, 0, 0)),
                pl.BlockSpec((FRAME, FRAME), lambda s, w: (0, 0)),
            ],
            out_specs=[pl.BlockSpec(memory_space=pl.ANY)] * 2,
            scratch_shapes=[
                pltpu.VMEM((2, per, 2 * FRAME, 128), BF16),
                pltpu.VMEM((per, 2, FRAME, 128), F32),
                pltpu.VMEM((groups, NOTE_ROWS, 128), BF16),
                pltpu.SMEM((frames + groups,), jnp.int32),
                pltpu.SemaphoreType.DMA((2 * per + 1,)),
            ],
        ),
        out_shape=[
            jax.ShapeDtypeStruct((groups, 2 * FRAME + NOTE_ROWS, 128), BF16),
            jax.ShapeDtypeStruct((groups, 2 * FRAME, 128), BF16),
        ],
        compiler_params=pltpu.CompilerParams(vmem_limit_bytes=56 << 20),
        cost_estimate=pl.CostEstimate(
            flops=frames * 2 * FRAME**3, bytes_accessed=frames * FRAME * FRAME * 6, transcendentals=0
        ),
        name="prep",
    )(where, intensity, jnp.asarray(deinterleave()))


def assemble_kernel(obj_ref, north_ref, south_ref, west_ref, east_ref, ext_ref):
    for part in range(2):
        ext_ref[part, 0] = west_ref[part].astype(F32)
        ext_ref[part, PANELS - 1] = east_ref[part].astype(F32)
        for j in range(TILE // 128):
            lanes = slice(128 * j, 128 * j + 128)
            ext_ref[part, j + 1, 0:HALF, :] = north_ref[part, :, lanes].astype(F32)
            ext_ref[part, j + 1, HALF : HALF + TILE, :] = obj_ref[part, :, lanes]
            ext_ref[part, j + 1, HALF + TILE :, :] = south_ref[part, :, lanes].astype(F32)


def assemble(obj, north, south, west, east):
    return pl.pallas_call(
        assemble_kernel,
        out_shape=jax.ShapeDtypeStruct((2, PANELS, EXTENT, 128), F32),
        compiler_params=pltpu.CompilerParams(vmem_limit_bytes=24 << 20),
        cost_estimate=pl.CostEstimate(flops=0, bytes_accessed=8 << 20, transcendentals=0),
        name="assemble",
    )(obj, north, south, west, east)


def rows_of(m, p=0, height=FRAME):
    return slice(FRAME * m + HALF * p, FRAME * m + HALF * p + height)


def forward(places, probe_ref, table_ref, ext_ref, xs, gs, take):
    members = range(len(places))
    lane = lax.broadcasted_iota(jnp.int32, (FRAME, 128), 1)
    for m in members:
        row, col, live = places[m]
        panel = col // 128
        shift = col % 128
        back_shift = (128 - shift) % 128
        keep = lane < 128 - shift

        def cut(part):
            rolled = [
                pltpu.roll(ext_ref[part, panel + i, pl.ds(row, FRAME), :], back_shift, 1)
                for i in range(3)
            ]
            return [jnp.where(keep, rolled[i], rolled[i + 1]) for i in range(2)]

        patch_re = cut(0)
        patch_im = cut(1)
        ex_re, ex_im = [], []
        for h in range(2):
            lanes = slice(128 * h, 128 * h + 128)
            pr = probe_ref[0, :, lanes]
            pi = probe_ref[1, :, lanes]
            ex_re.append(pr * patch_re[h] - pi * patch_im[h])
            ex_im.append(pr * patch_im[h] + pi * patch_re[h])
        xs[0, rows_of(m), 0:128] = (ex_re[0] + ex_re[1]).astype(BF16)
        xs[0, rows_of(m), 128:256] = (ex_im[0] + ex_im[1]).astype(BF16)
        xs[1, rows_of(m), 0:128] = (ex_re[0] - ex_re[1]).astype(BF16)
        xs[1, rows_of(m), 128:256] = (ex_im[0] - ex_im[1]).astype(BF16)
    halves = [dot(xs[q], table_ref[q]) for q in range(2)]
    for m in members:
        for q in range(2):
            half = halves[q][rows_of(m)]
            top, bottom = half[:HALF], half[HALF:]
            lanes = slice(128 * q, 128 * q + 128)
            for p, fold in ((0, top + bottom), (1, top - bottom)):
                folded = fold.astype(BF16)
                gs[m, p, 0:HALF, lanes] = folded[:, :128]
                gs[m, p, HALF:, lanes] = folded[:, 128:]
    for m in members:
        for p in range(2):
            take(m, p, dot(table_ref[2 + p], gs[m, p]))


def update(m, p, far, amp_ref, ds):
    for q in range(2):
        lanes = slice(128 * q, 128 * q + 128)
        far_re, far_im = far[:HALF, lanes], far[HALF:, lanes]
        a = amp_ref[m, FRAME * q + HALF * p : FRAME * q + HALF * p + HALF, :].astype(F32)
        factor = a * lax.rsqrt(far_re * far_re + far_im * far_im + 1.0) - 1.0
        ds[q, rows_of(m, p, HALF), 0:128] = (far_re * factor).astype(BF16)
        ds[q, rows_of(m, p, HALF), 128:256] = (far_im * factor).astype(BF16)


def backward(places, probe_ref, table_ref, acc_ref, ds, ms):
    members = range(len(places))
    lane = lax.broadcasted_iota(jnp.int32, (HALF, 128), 1)
    evens = dot(ds[0], table_ref[4])
    odds = dot(ds[1], table_ref[5])
    for m in members:
        even, odd = evens[rows_of(m)], odds[rows_of(m)]
        for h, mid in ((0, (even + odd).astype(BF16)), (1, (even - odd).astype(BF16))):
            lanes = slice(128 * h, 128 * h + 128)
            for p in range(2):
                rows = slice(HALF * p, HALF * p + HALF)
                ms[m, p, 0:HALF, lanes] = mid[rows, :128]
                ms[m, p, HALF:, lanes] = mid[rows, 128:]
    for m in members:
        row, col, live = places[m]
        shift = col % 128
        panel = jnp.where(live > 0, col // 128, PANELS)
        even = dot(table_ref[6], ms[m, 0])
        odd = dot(table_ref[7], ms[m, 1])
        keep = lane < shift
        for v in range(2):
            back = even + odd if v == 0 else even - odd
            back_re, back_im = back[:HALF], back[HALF:]
            rows = slice(HALF * v, HALF * v + HALF)
            pr = probe_ref[0, rows]
            pi = probe_ref[1, rows]
            where = pl.ds(row + HALF * v, HALF)
            for part, term in ((0, pr * back_re + pi * back_im), (1, pr * back_im - pi * back_re)):
                left = pltpu.roll(term[:, :128], shift, 1)
                right = pltpu.roll(term[:, 128:], shift, 1)
                acc_ref[part, panel, where, :] += jnp.where(keep, 0.0, left)
                acc_ref[part, panel + 1, where, :] += jnp.where(keep, left, right)
                acc_ref[part, panel + 2, where, :] += jnp.where(keep, right, 0.0)


def places_of(meta_ref, rank, group):
    places = [[meta_ref[3 * rank + k, group * GROUP + m] for k in range(3)] for m in range(GROUP)]
    live = places[0][2]
    for place in places[1:]:
        live = live + place[2]
    return places, live > 0


def first_kernel(
    meta_ref, amp_ref, probe_ref, table_ref, ext_ref, out_ref, far_ref, acc_ref, xs, gs, ds, ms
):
    step = pl.program_id(0)
    groups = pl.num_programs(0) // 2

    @pl.when(step == 0)
    def _():
        acc_ref[:, 0:PANELS] = jnp.zeros_like(out_ref)

    places, live = places_of(meta_ref, 0, jnp.minimum(step, groups - 1))

    @pl.when(live & (step < groups))
    def _():
        def take(m, p, far):
            update(m, p, far, amp_ref, ds)

        forward(places, probe_ref, table_ref, ext_ref, xs, gs, take)
        backward(places, probe_ref, table_ref, acc_ref, ds, ms)

    @pl.when(step == groups - 1)
    def _():
        out_ref[...] = acc_ref[:, 0:PANELS]

    later, live = places_of(meta_ref, 1, jnp.maximum(step - groups, 0))

    @pl.when(live & (step >= groups))
    def _():
        def take(m, p, far):
            far_ref[m, p] = far

        forward(later, probe_ref, table_ref, ext_ref, xs, gs, take)


def last_kernel(
    meta_ref, amp_ref, far_ref, probe_ref, table_ref, start_hbm, obj_hbm,
    west_ref, east_ref, mid_ref, acc_ref, start_ref, obj_ref, sems, ds, ms,
):
    step = pl.program_id(0)

    def loads():
        return [
            pltpu.make_async_copy(start_hbm, start_ref, sems.at[0]),
            pltpu.make_async_copy(obj_hbm, obj_ref, sems.at[1]),
        ]

    @pl.when(step == 0)
    def _():
        for copy in loads():
            copy.start()
        acc_ref[:, 0:PANELS] = jnp.zeros_like(start_ref)

    places, live = places_of(meta_ref, 1, step)

    @pl.when(live)
    def _():
        for m in range(GROUP):
            for p in range(2):
                update(m, p, far_ref[m, p], amp_ref, ds)
        backward(places, probe_ref, table_ref, acc_ref, ds, ms)

    @pl.when(step == pl.num_programs(0) - 1)
    def _():
        for copy in loads():
            copy.wait()

        def half_sum(part, panel, rows):
            return 0.5 * (acc_ref[part, panel, rows, :] + start_ref[part, panel, rows, :])

        for part in range(2):
            west_ref[part] = half_sum(part, 0, slice(0, EXTENT)).astype(BF16)
            east_ref[part] = half_sum(part, PANELS - 1, slice(0, EXTENT)).astype(BF16)
            for j in range(TILE // 128):
                lanes = slice(128 * j, 128 * j + 128)
                inner = slice(HALF, HALF + TILE)
                for rows in (slice(0, HALF), slice(HALF + TILE, EXTENT)):
                    mid_ref[part, rows, lanes] = half_sum(part, j + 1, rows)
                mid_ref[part, inner, lanes] = obj_ref[part, :, lanes] + half_sum(part, j + 1, inner)


def whole(shape):
    return pl.BlockSpec(shape, lambda s, m: (0,) * len(shape))


WIDE = (2, PANELS, EXTENT, 128)
SUMS = (2, PANELS + 3, EXTENT, 128)
FLAT = (2, GROUP * FRAME, FRAME)
DEEP = (GROUP, 2, FRAME, FRAME)


def run_first(meta, amps, probe, tabs, ext):
    groups = amps.shape[0] // GROUP
    return pl.pallas_call(
        first_kernel,
        grid_spec=pltpu.PrefetchScalarGridSpec(
            num_scalar_prefetch=1,
            grid=(2 * groups,),
            in_specs=[
                pl.BlockSpec(
                    (GROUP,) + amps.shape[1:], lambda s, m: (jnp.minimum(s, groups - 1), 0, 0)
                ),
                whole((2, FRAME, FRAME)),
                whole((8, FRAME, FRAME)),
                whole(WIDE),
            ],
            out_specs=[
                whole(WIDE),
                pl.BlockSpec(DEEP, lambda s, m: (jnp.maximum(s - groups, 0), 0, 0, 0)),
            ],
            scratch_shapes=[pltpu.VMEM(SUMS, F32)]
            + [pltpu.VMEM(shape, BF16) for shape in (FLAT, DEEP, FLAT, DEEP)],
        ),
        out_shape=[
            jax.ShapeDtypeStruct(WIDE, F32),
            jax.ShapeDtypeStruct((amps.shape[0], 2, FRAME, FRAME), F32),
        ],
        compiler_params=pltpu.CompilerParams(vmem_limit_bytes=56 << 20),
        cost_estimate=pl.CostEstimate(
            flops=2 * amps.shape[0] * 16 * FRAME**3, bytes_accessed=24 << 20, transcendentals=0
        ),
        name="first",
    )(meta, amps, probe, tabs, ext)


def run_last(meta, amps, far, probe, tabs, start, obj):
    groups = amps.shape[0] // GROUP
    shapes = [(2, EXTENT, 128), (2, EXTENT, 128), (2, EXTENT, TILE)]
    return pl.pallas_call(
        last_kernel,
        grid_spec=pltpu.PrefetchScalarGridSpec(
            num_scalar_prefetch=1,
            grid=(groups,),
            in_specs=[
                pl.BlockSpec((GROUP,) + amps.shape[1:], lambda s, m: (s, 0, 0)),
                pl.BlockSpec(DEEP, lambda s, m: (s, 0, 0, 0)),
                whole((2, FRAME, FRAME)),
                whole((8, FRAME, FRAME)),
                pl.BlockSpec(memory_space=pl.ANY),
                pl.BlockSpec(memory_space=pl.ANY),
            ],
            out_specs=[whole(shape) for shape in shapes],
            scratch_shapes=[
                pltpu.VMEM(SUMS, F32),
                pltpu.VMEM(WIDE, F32),
                pltpu.VMEM((2, TILE, TILE), F32),
                pltpu.SemaphoreType.DMA((2,)),
                pltpu.VMEM(FLAT, BF16),
                pltpu.VMEM(DEEP, BF16),
            ],
        ),
        out_shape=[jax.ShapeDtypeStruct(s, d) for s, d in zip(shapes, (BF16, BF16, F32))],
        compiler_params=pltpu.CompilerParams(vmem_limit_bytes=56 << 20),
        cost_estimate=pl.CostEstimate(
            flops=amps.shape[0] * 8 * FRAME**3, bytes_accessed=20 << 20, transcendentals=0
        ),
        name="last",
    )(meta, amps, far, probe, tabs, start, obj)


def finish_kernel(base_ref, north_ref, south_ref, out_ref):
    @pl.when(pl.program_id(0) == 0)
    def _():
        out_ref[...] = base_ref[...] + north_ref[...].astype(F32)

    @pl.when(pl.program_id(0) == 1)
    def _():
        out_ref[...] = base_ref[...] + south_ref[...].astype(F32)


def shifted(value, axis, by):
    size = lax.axis_size(axis)
    pairs = [(i, i + by) for i in range(size) if 0 <= i + by < size]
    return lax.ppermute(value, axis, pairs)


def body(obj, probe, intensity, dest, offsets):
    groups = lax.axis_size("gx")
    sends = prep(jnp.concatenate([dest.T, offsets.T]).reshape(-1), intensity, groups)
    north = shifted(obj[:, TILE - HALF :, :].astype(BF16), "gy", 1)
    south = shifted(obj[:, :HALF, :].astype(BF16), "gy", -1)
    routed = functools.partial(
        lax.all_to_all, axis_name="gx", split_axis=0, concat_axis=0, tiled=True
    )
    amps = routed(sends[0])

    def column(lo, hi):
        own = obj[:, :, lo:hi].astype(BF16)
        return jnp.concatenate([north[:, :, lo:hi], own, south[:, :, lo:hi]], axis=1)

    west = shifted(column(TILE - HALF, TILE), "gx", 1)
    east = shifted(column(0, HALF), "gx", -1)
    west, east, rest = lax.optimization_barrier((west, east, sends[1]))
    more = routed(rest)
    ext = assemble(obj, north, south, west, east)
    tabs = jnp.asarray(table_blocks())
    notes = amps[:, 2 * FRAME, :10].astype(jnp.int32).T
    meta = jnp.stack(
        [
            notes[5 * r] * 16 + notes[5 * r + 1] if k == 0 else
            notes[5 * r + 2] * 16 + notes[5 * r + 3] if k == 1 else notes[5 * r + 4]
            for r in range(CAP) for k in range(3)
        ]
    )
    acc, far = run_first(meta, amps, probe, tabs, ext)
    west, east, mid = run_last(meta, more, far, probe, tabs, acc, obj)
    from_west = shifted(east, "gx", 1).astype(F32)
    from_east = shifted(west, "gx", -1).astype(F32)

    def summed(lo, hi):
        rows = mid[:, lo:hi]
        left = rows[:, :, :HALF] + from_west[:, lo:hi]
        right = rows[:, :, TILE - HALF :] + from_east[:, lo:hi]
        return jnp.concatenate([left, rows[:, :, HALF : TILE - HALF], right], axis=2)

    to_north = summed(0, HALF).astype(BF16)
    to_south = summed(HALF + TILE, EXTENT).astype(BF16)
    from_north = shifted(to_south, "gy", 1)
    from_south = shifted(to_north, "gy", -1)
    inner = summed(HALF, HALF + TILE)
    return pl.pallas_call(
        finish_kernel,
        grid=(2,),
        in_specs=[
            pl.BlockSpec((2, HALF, TILE), lambda i: (0, 3 * i, 0)),
            pl.BlockSpec((2, HALF, TILE), lambda i: (0, 0, 0)),
            pl.BlockSpec((2, HALF, TILE), lambda i: (0, 0, 0)),
        ],
        out_specs=pl.BlockSpec((2, HALF, TILE), lambda i: (0, 3 * i, 0)),
        out_shape=jax.ShapeDtypeStruct((2, TILE, TILE), F32),
        input_output_aliases={0: 0},
        name="finish",
    )(inner, from_north, from_south)


def solution(mesh):
    placed = (
        P(None, "gy", "gx"),
        P(),
        P(("gx", "gy"), None, None),
        P(("gx", "gy"), None),
        P(("gx", "gy"), None),
    )
    return jax.shard_map(
        body, mesh=mesh, in_specs=placed, out_specs=P(None, "gy", "gx"), check_vma=False
    )
```

time: 161 us -> 151 us (0.938)
  the two profiles are of different devices: /device:TPU:105 before, /device:TPU:19 now
where the time goes in v2:
time: 151 us; the launch traced here: 150 us
  waiting for transfers between devices  55.1 us (36%)
  Pallas kernels  47.7 us (32%)
  starting transfers between devices  35.2 us (23%)
  local copies, waits for them, and re-layouts  6.39 us (4%)
  other arithmetic  5.09 us (3%)
    ppermute x8, waiting for transfers between devices, shifted(): return lax.ppermute(value, axis, pairs)  55.1 us
    pallas_call x1, Pallas kernels, run_first(): pl.pallas_call(first_kernel, grid_spec=pltpu.PrefetchScalarGridSpec(num_s...  25.9 us
    ppermute x8, starting transfers between devices, shifted(): return lax.ppermute(value, axis, pairs)  21.8 us
    pallas_call x1, Pallas kernels, run_last(): pl.pallas_call(last_kernel, grid_spec=pltpu.PrefetchScalarGridSpec(num_sc...  13.2 us
    all_to_all x1, starting transfers between devices, body(): amps = routed(sends[0])  6.84 us
    all_to_all x1, starting transfers between devices, body(): more = routed(rest)  6.48 us
    pallas_call x1, Pallas kernels, prep(): pl.pallas_call(prep_kernel, grid_spec=pltpu.PrefetchScalarGridSpec(num_sc...  6.14 us
  transfers between devices with their start and end apart: 10, of which 8 were waited for; matrix products, arithmetic and copies ran while one was open for 5% of the time, Pallas kernels for 18%

profile of v2, /device:TPU:19, one launch (start us, length us, event | category | flops | bytes accessed | tf_op | source)
XLA Modules:
  0.0 149.7 jit_solution(7534324100208360177)
XLA Ops:
  0.0 0.7 pad_add_fusion
  0.7 0.6 reshape.5.where_ref
  1.3 6.1 %prep.1 = (bf16[16,528,128]{2,1,0:T(8,128)(2,1)}, bf16[16,512,128]{2,1,0:T(8,128)(2,1)}) custom-call(s32[48]{0:T(128)} %reshape.5.where_ref, f32[16,256,256]{2,1,0:T(8,128)} %inten_ref.1, bf16[256,256]{1,0:T(8,128)(2,1)} %constant.6.clone.perm_ref), custom_call_target="tpu_custom_call" | custom-call | flops 536870912 | bytes 6291456 | tf_op jit(solution)/shard_map/prep/pallas_call | solution.py:140
  7.4 0.0 copy-start
  7.5 6.8 %all-to-all-start = ((bf16[16,528,128]{2,1,0:T(8,128)(2,1)}), bf16[16,528,128]{2,1,0:T(8,128)(2,1)}, u32[]{:S(2)}, u32[]{:S(2)}) async-start(bf16[16,528,128]{2,1,0:T(8,128)(2,1)} %get-tuple-element.15), calls=%async_computation | async-start | bytes 4325376 | tf_op jit(solution)/shard_map/all_to_all | solution.py:476
  14.3 0.0 copy-done
  14.3 0.1 convert.26
  14.5 4.4 %collective-permute-start = (bf16[2,128,512]{2,1,0:T(8,128)(2,1)S(1)}, bf16[2,128,512]{2,1,0:T(8,128)(2,1)S(1)}, u32[]{:S(2)}, u32[]{:S(2)}) collective-permute-start(bf16[2,128,512]{2,1,0:T(8,128)(2,1)S(1)} %get-tuple-element.37), channel_id=1, source_target_pairs={{0,1},{1,2},{2,3},{3,4},{4,5},{5,6},{6,7},{8,9},{9,10},{10,11},{11... | collective-permute-start | bytes 786440 | tf_op jit(solution)/shard_map/ppermute | solution.py:465
  18.9 1.9 %collective-permute-start.1 = (bf16[2,128,512]{2,1,0:T(8,128)(2,1)S(1)}, bf16[2,128,512]{2,1,0:T(8,128)(2,1)S(1)}, u32[]{:S(2)}, u32[]{:S(2)}) collective-permute-start(bf16[2,128,512]{2,1,0:T(8,128)(2,1)S(1)} %get-tuple-element.38), channel_id=1, source_target_pairs={{1,0},{2,1},{3,2},{4,3},{5,4},{6,5},{7,6},{9,8},{10,9},{11,10},{12... | collective-permute-start | bytes 786440 | tf_op jit(solution)/shard_map/ppermute | solution.py:465
  20.8 0.1 fusion.5
  20.9 25.3 %collective-permute-done.north_ref = bf16[2,128,512]{2,1,0:T(8,128)(2,1)S(1)} collective-permute-done((bf16[2,128,512]{2,1,0:T(8,128)(2,1)S(1)}, bf16[2,128,512]{2,1,0:T(8,128)(2,1)S(1)}, u32[]{:S(2)}, u32[]{:S(2)}) %collective-permute-start) | collective-permute-done | bytes 262176 | tf_op jit(solution)/shard_map/ppermute | solution.py:465
  46.2 6.9 %collective-permute-done.1.south_ref = bf16[2,128,512]{2,1,0:T(8,128)(2,1)S(1)} collective-permute-done((bf16[2,128,512]{2,1,0:T(8,128)(2,1)S(1)}, bf16[2,128,512]{2,1,0:T(8,128)(2,1)S(1)}, u32[]{:S(2)}, u32[]{:S(2)}) %collective-permute-start.1) | collective-permute-done | bytes 262176 | tf_op jit(solution)/shard_map/ppermute | solution.py:465
  53.2 4.0 %collective-permute-start.2 = (bf16[2,768,128]{2,1,0:T(8,128)(2,1)S(1)}, bf16[2,768,128]{2,1,0:T(8,128)(2,1)S(1)}, u32[]{:S(2)}, u32[]{:S(2)}) collective-permute-start(bf16[2,768,128]{2,1,0:T(8,128)(2,1)S(1)} %pad_maximum_fusion.1), channel_id=1, source_target_pairs={{0,8},{8,16},{16,24},{24,32},{32,40},{40,48},{48,56},{56,64},{64,7... | collective-permute-start | bytes 1179656 | tf_op jit(solution)/shard_map/ppermute | solution.py:465
  57.2 1.9 %collective-permute-start.3 = (bf16[2,768,128]{2,1,0:T(8,128)(2,1)S(1)}, bf16[2,768,128]{2,1,0:T(8,128)(2,1)S(1)}, u32[]{:S(2)}, u32[]{:S(2)}) collective-permute-start(bf16[2,768,128]{2,1,0:T(8,128)(2,1)S(1)} %pad_maximum_fusion.2), channel_id=1, source_target_pairs={{8,0},{16,8},{24,16},{32,24},{40,32},{48,40},{56,48},{64,56},{72,6... | collective-permute-start | bytes 1179656 | tf_op jit(solution)/shard_map/ppermute | solution.py:465
  59.2 2.7 %collective-permute-done.2.west_ref = bf16[2,768,128]{2,1,0:T(8,128)(2,1)S(1)} collective-permute-done((bf16[2,768,128]{2,1,0:T(8,128)(2,1)S(1)}, bf16[2,768,128]{2,1,0:T(8,128)(2,1)S(1)}, u32[]{:S(2)}, u32[]{:S(2)}) %collective-permute-start.2) | collective-permute-done | bytes 393248 | tf_op jit(solution)/shard_map/ppermute | solution.py:465
  61.9 6.3 %collective-permute-done.3.east_ref = bf16[2,768,128]{2,1,0:T(8,128)(2,1)S(1)} collective-permute-done((bf16[2,768,128]{2,1,0:T(8,128)(2,1)S(1)}, bf16[2,768,128]{2,1,0:T(8,128)(2,1)S(1)}, u32[]{:S(2)}, u32[]{:S(2)}) %collective-permute-start.3) | collective-permute-done | bytes 393248 | tf_op jit(solution)/shard_map/ppermute | solution.py:465
  68.2 0.0 all-to-all-done.amp_ref
  68.2 6.5 %all-to-all-start.1 = ((bf16[16,512,128]{2,1,0:T(8,128)(2,1)}), bf16[16,512,128]{2,1,0:T(8,128)(2,1)}, u32[]{:S(2)}, u32[]{:S(2)}) async-start(bf16[16,512,128]{2,1,0:T(8,128)(2,1)} %get-tuple-element.17), calls=%async_computation.1 | async-start | bytes 4194304 | tf_op jit(solution)/shard_map/all_to_all | solution.py:485
  74.7 0.3 assemble.1.ext_ref
  75.0 0.0 copy-start.1
  75.0 2.1 %copy-done.1 = f32[2,6,768,128]{3,2,1,0:T(8,128)} copy-done((f32[2,6,768,128]{3,2,1,0:T(8,128)}, f32[2,6,768,128]{3,2,1,0:T(8,128)S(1)}, u32[]{:S(2)}) %copy-start.1) | copy-done | bytes 4718616
  77.1 0.8 slice.154
  77.8 0.1 copy.12
  78.0 0.6 stack.2.meta_ref
  78.6 25.9 %first.1 = (f32[2,6,768,128]{3,2,1,0:T(8,128)}, f32[16,2,256,256]{3,2,1,0:T(8,128)}) custom-call(s32[6,16]{1,0:T(8,128)} %stack.2.meta_ref, bf16[16,528,128]{2,1,0:T(8,128)(2,1)} %all-to-all-done.amp_ref, f32[2,256,256]{2,1,0:T(8,128)} %probe_ref.3, bf16[8,256,256]{2,1,0:T(8,128)(2,1)} %constant.7.clone.table_ref, f32[2,6,768,128]{3,2,1,0:T(8,128)} %copy-done.1), custom_call_target="tpu_custom_call" | custom-call | flops 8589934592 | bytes 25165824 | tf_op jit(solution)/shard_map/first/pallas_call | solution.py:385
  104.5 0.0 all-to-all-done.1.amp_ref
  104.5 13.2 %last.1 = (bf16[2,768,128]{2,1,0:T(8,128)(2,1)}, bf16[2,768,128]{2,1,0:T(8,128)(2,1)}, f32[2,768,512]{2,1,0:T(8,128)}) custom-call(s32[6,16]{1,0:T(8,128)} %stack.2.meta_ref, bf16[16,512,128]{2,1,0:T(8,128)(2,1)} %all-to-all-done.1.amp_ref, f32[16,2,256,256]{3,2,1,0:T(8,128)} %get-tuple-element.20.far_ref, f32[2,256,256]{2,1,0:T(8,128)} %probe_ref.3, ...), custom_call_target="tpu_custom_call" | custom-call | flops 2147483648 | bytes 20971520 | tf_op jit(solution)/shard_map/last/pallas_call | solution.py:420
  117.7 1.9 %collective-permute-start.4 = (bf16[2,768,128]{2,1,0:T(8,128)(2,1)}, bf16[2,768,128]{2,1,0:T(8,128)(2,1)S(1)}, u32[]{:S(2)}, u32[]{:S(2)}) collective-permute-start(bf16[2,768,128]{2,1,0:T(8,128)(2,1)} %get-tuple-element.23), channel_id=1, source_target_pairs={{0,8},{8,16},{16,24},{24,32},{32,40},{40,48},{48,56},{56,64},{64,7... | collective-permute-start | bytes 1179656 | tf_op jit(solution)/shard_map/ppermute | solution.py:465
  119.6 2.4 %collective-permute-start.5 = (bf16[2,768,128]{2,1,0:T(8,128)(2,1)}, bf16[2,768,128]{2,1,0:T(8,128)(2,1)S(1)}, u32[]{:S(2)}, u32[]{:S(2)}) collective-permute-start(bf16[2,768,128]{2,1,0:T(8,128)(2,1)} %get-tuple-element.24), channel_id=1, source_target_pairs={{8,0},{16,8},{24,16},{32,24},{40,32},{48,40},{56,48},{64,56},{72,6... | collective-permute-start | bytes 1179656 | tf_op jit(solution)/shard_map/ppermute | solution.py:465
  122.0 1.3 slice.141
  123.3 0.0 copy-start.2
  123.3 2.2 %convert.28 = bf16[2,768,512]{2,1,0:T(8,128)(2,1)S(1)} convert(f32[2,768,512]{2,1,0:T(8,128)} %get-tuple-element.22) | non-fusion elementwise | flops 786432 | bytes 4718592 | tf_op jit(solution)/shard_map/convert.9
  125.6 0.5 collective-permute-done.4
  126.2 0.1 convert_element_type.8
  126.2 4.2 %collective-permute-done.5 = bf16[2,768,128]{2,1,0:T(8,128)(2,1)S(1)} collective-permute-done((bf16[2,768,128]{2,1,0:T(8,128)(2,1)}, bf16[2,768,128]{2,1,0:T(8,128)(2,1)S(1)}, u32[]{:S(2)}, u32[]{:S(2)}) %collective-permute-start.5) | collective-permute-done | bytes 393248 | tf_op jit(solution)/shard_map/ppermute | solution.py:465
  130.4 0.1 convert_element_type.18
  130.5 0.0 copy-done.2
  130.5 0.1 fusion.1
  130.6 3.3 %collective-permute-start.6 = (bf16[2,128,512]{2,1,0:T(8,128)(2,1)S(1)}, bf16[2,128,512]{2,1,0:T(8,128)(2,1)S(1)}, u32[]{:S(2)}, u32[]{:S(2)}) collective-permute-start(bf16[2,128,512]{2,1,0:T(8,128)(2,1)S(1)} %pad_maximum_fusion.3), channel_id=1, source_target_pairs={{0,1},{1,2},{2,3},{3,4},{4,5},{5,6},{6,7},{8,9},{9,10},{10,11},{11... | collective-permute-start | bytes 786440 | tf_op jit(solution)/shard_map/ppermute | solution.py:465
  134.0 2.0 %collective-permute-start.7 = (bf16[2,128,512]{2,1,0:T(8,128)(2,1)S(1)}, bf16[2,128,512]{2,1,0:T(8,128)(2,1)S(1)}, u32[]{:S(2)}, u32[]{:S(2)}) collective-permute-start(bf16[2,128,512]{2,1,0:T(8,128)(2,1)S(1)} %pad_maximum_fusion.4), channel_id=1, source_target_pairs={{1,0},{2,1},{3,2},{4,3},{5,4},{6,5},{7,6},{9,8},{10,9},{11,10},{12... | collective-permute-start | bytes 786440 | tf_op jit(solution)/shard_map/ppermute | solution.py:465
  135.9 0.1 slice_add_fusion.1
  136.1 1.5 %pad_maximum_fusion.base_ref = f32[2,512,512]{2,1,0:T(8,128)} fusion(f32[2,512,128]{2,1,0:T(8,128)S(1)} %get-tuple-element.32, f32[2,512,256]{2,1,0:T(8,128)S(1)} %slice.141, f32[2,512,128]{2,1,0:T(8,128)S(1)} %get-tuple-element.31), kind=kLoop, calls=%fused_computation | loop fusion | flops 1048576 | bytes 4194304 | tf_op jit(solution)/shard_map/concatenate | solution.py:505
  137.6 2.3 %collective-permute-done.6.north_ref = bf16[2,128,512]{2,1,0:T(8,128)(2,1)S(1)} collective-permute-done((bf16[2,128,512]{2,1,0:T(8,128)(2,1)S(1)}, bf16[2,128,512]{2,1,0:T(8,128)(2,1)S(1)}, u32[]{:S(2)}, u32[]{:S(2)}) %collective-permute-start.6) | collective-permute-done | bytes 262176 | tf_op jit(solution)/shard_map/ppermute | solution.py:465
  140.0 0.0 copy-start.3
  140.0 6.8 %collective-permute-done.7.south_ref = bf16[2,128,512]{2,1,0:T(8,128)(2,1)S(1)} collective-permute-done((bf16[2,128,512]{2,1,0:T(8,128)(2,1)S(1)}, bf16[2,128,512]{2,1,0:T(8,128)(2,1)S(1)}, u32[]{:S(2)}, u32[]{:S(2)}) %collective-permute-start.7) | collective-permute-done | bytes 262176 | tf_op jit(solution)/shard_map/ppermute | solution.py:465
  146.8 0.0 copy-done.3
  146.8 0.7 copy-done.4
  147.5 2.2 %finish.1 = f32[2,512,512]{2,1,0:T(8,128)} custom-call(f32[2,512,512]{2,1,0:T(8,128)} %pad_maximum_fusion.base_ref, bf16[2,128,512]{2,1,0:T(8,128)(2,1)} %copy-done.3, bf16[2,128,512]{2,1,0:T(8,128)(2,1)} %copy-done.4), custom_call_target="tpu_custom_call", output_to_operand_aliasing={{}: (0, {})} | custom-call | tf_op jit(solution)/shard_map/finish/pallas_call | solution.py:512
  (11 shorter events, 0.3 us)
Async XLA Ops:
  7.4 6.9 %copy-start = (f32[2,512,512]{2,1,0:T(8,128)S(1)}, f32[2,512,512]{2,1,0:T(8,128)}, u32[]{:S(2)}) copy-start(f32[2,512,512]{2,1,0:T(8,128)} %obj_hbm.1) | copy-start | bytes 6291460
  7.5 60.7 %all-to-all-start = ((bf16[16,528,128]{2,1,0:T(8,128)(2,1)}), bf16[16,528,128]{2,1,0:T(8,128)(2,1)}, u32[]{:S(2)}, u32[]{:S(2)}) async-start(bf16[16,528,128]{2,1,0:T(8,128)(2,1)} %get-tuple-element.15), calls=%async_computation | async-start | bytes 4325376 | tf_op jit(solution)/shard_map/all_to_all | solution.py:476
  14.5 31.7 %collective-permute-start = (bf16[2,128,512]{2,1,0:T(8,128)(2,1)S(1)}, bf16[2,128,512]{2,1,0:T(8,128)(2,1)S(1)}, u32[]{:S(2)}, u32[]{:S(2)}) collective-permute-start(bf16[2,128,512]{2,1,0:T(8,128)(2,1)S(1)} %get-tuple-element.37), channel_id=1, source_target_pairs={{0,1},{1,2},{2,3},{3,4},{4,5},{5,6},{6,7},{8,9},{9,10},{10,11},{11... | collective-permute-start | bytes 786440 | tf_op jit(solution)/shard_map/ppermute | solution.py:465
  18.9 34.3 %collective-permute-start.1 = (bf16[2,128,512]{2,1,0:T(8,128)(2,1)S(1)}, bf16[2,128,512]{2,1,0:T(8,128)(2,1)S(1)}, u32[]{:S(2)}, u32[]{:S(2)}) collective-permute-start(bf16[2,128,512]{2,1,0:T(8,128)(2,1)S(1)} %get-tuple-element.38), channel_id=1, source_target_pairs={{1,0},{2,1},{3,2},{4,3},{5,4},{6,5},{7,6},{9,8},{10,9},{11,10},{12... | collective-permute-start | bytes 786440 | tf_op jit(solution)/shard_map/ppermute | solution.py:465
  53.2 8.7 %collective-permute-start.2 = (bf16[2,768,128]{2,1,0:T(8,128)(2,1)S(1)}, bf16[2,768,128]{2,1,0:T(8,128)(2,1)S(1)}, u32[]{:S(2)}, u32[]{:S(2)}) collective-permute-start(bf16[2,768,128]{2,1,0:T(8,128)(2,1)S(1)} %pad_maximum_fusion.1), channel_id=1, source_target_pairs={{0,8},{8,16},{16,24},{24,32},{32,40},{40,48},{48,56},{56,64},{64,7... | collective-permute-start | bytes 1179656 | tf_op jit(solution)/shard_map/ppermute | solution.py:465
  57.2 10.9 %collective-permute-start.3 = (bf16[2,768,128]{2,1,0:T(8,128)(2,1)S(1)}, bf16[2,768,128]{2,1,0:T(8,128)(2,1)S(1)}, u32[]{:S(2)}, u32[]{:S(2)}) collective-permute-start(bf16[2,768,128]{2,1,0:T(8,128)(2,1)S(1)} %pad_maximum_fusion.2), channel_id=1, source_target_pairs={{8,0},{16,8},{24,16},{32,24},{40,32},{48,40},{56,48},{64,56},{72,6... | collective-permute-start | bytes 1179656 | tf_op jit(solution)/shard_map/ppermute | solution.py:465
  68.2 36.3 %all-to-all-start.1 = ((bf16[16,512,128]{2,1,0:T(8,128)(2,1)}), bf16[16,512,128]{2,1,0:T(8,128)(2,1)}, u32[]{:S(2)}, u32[]{:S(2)}) async-start(bf16[16,512,128]{2,1,0:T(8,128)(2,1)} %get-tuple-element.17), calls=%async_computation.1 | async-start | bytes 4194304 | tf_op jit(solution)/shard_map/all_to_all | solution.py:485
  75.0 2.1 %copy-start.1 = (f32[2,6,768,128]{3,2,1,0:T(8,128)}, f32[2,6,768,128]{3,2,1,0:T(8,128)S(1)}, u32[]{:S(2)}) copy-start(f32[2,6,768,128]{3,2,1,0:T(8,128)S(1)} %assemble.1.ext_ref) | copy-start | bytes 14155780
  117.7 8.5 %collective-permute-start.4 = (bf16[2,768,128]{2,1,0:T(8,128)(2,1)}, bf16[2,768,128]{2,1,0:T(8,128)(2,1)S(1)}, u32[]{:S(2)}, u32[]{:S(2)}) collective-permute-start(bf16[2,768,128]{2,1,0:T(8,128)(2,1)} %get-tuple-element.23), channel_id=1, source_target_pairs={{0,8},{8,16},{16,24},{24,32},{32,40},{40,48},{48,56},{56,64},{64,7... | collective-permute-start | bytes 1179656 | tf_op jit(solution)/shard_map/ppermute | solution.py:465
  119.6 10.8 %collective-permute-start.5 = (bf16[2,768,128]{2,1,0:T(8,128)(2,1)}, bf16[2,768,128]{2,1,0:T(8,128)(2,1)S(1)}, u32[]{:S(2)}, u32[]{:S(2)}) collective-permute-start(bf16[2,768,128]{2,1,0:T(8,128)(2,1)} %get-tuple-element.24), channel_id=1, source_target_pairs={{8,0},{16,8},{24,16},{32,24},{40,32},{48,40},{56,48},{64,56},{72,6... | collective-permute-start | bytes 1179656 | tf_op jit(solution)/shard_map/ppermute | solution.py:465
  123.3 7.1 %copy-start.2 = (f32[2,768,512]{2,1,0:T(8,128)S(1)}, f32[2,768,512]{2,1,0:T(8,128)}, u32[]{:S(2)}) copy-start(f32[2,768,512]{2,1,0:T(8,128)} %get-tuple-element.22) | copy-start | bytes 9437188
  130.6 9.4 %collective-permute-start.6 = (bf16[2,128,512]{2,1,0:T(8,128)(2,1)S(1)}, bf16[2,128,512]{2,1,0:T(8,128)(2,1)S(1)}, u32[]{:S(2)}, u32[]{:S(2)}) collective-permute-start(bf16[2,128,512]{2,1,0:T(8,128)(2,1)S(1)} %pad_maximum_fusion.3), channel_id=1, source_target_pairs={{0,1},{1,2},{2,3},{3,4},{4,5},{5,6},{6,7},{8,9},{9,10},{10,11},{11... | collective-permute-start | bytes 786440 | tf_op jit(solution)/shard_map/ppermute | solution.py:465
  134.0 12.8 %collective-permute-start.7 = (bf16[2,128,512]{2,1,0:T(8,128)(2,1)S(1)}, bf16[2,128,512]{2,1,0:T(8,128)(2,1)S(1)}, u32[]{:S(2)}, u32[]{:S(2)}) collective-permute-start(bf16[2,128,512]{2,1,0:T(8,128)(2,1)S(1)} %pad_maximum_fusion.4), channel_id=1, source_target_pairs={{1,0},{2,1},{3,2},{4,3},{5,4},{6,5},{7,6},{9,8},{10,9},{11,10},{12... | collective-permute-start | bytes 786440 | tf_op jit(solution)/shard_map/ppermute | solution.py:465
  140.0 6.8 %copy-start.3 = (bf16[2,128,512]{2,1,0:T(8,128)(2,1)}, bf16[2,128,512]{2,1,0:T(8,128)(2,1)S(1)}, u32[]{:S(2)}) copy-start(bf16[2,128,512]{2,1,0:T(8,128)(2,1)S(1)} %collective-permute-done.6.north_ref) | copy-start | bytes 786436
  146.8 0.7 copy-start.4
